TPU v7x, 32 devices: a whole 2x2x4 slice. The times are simulated.
32 devices in a mesh: gx: 16 (over z, x, core), gy: 2 (over y).
Axes of the slice: x: 2, y: 2, z: 4, core: 2. Of those that a mesh axis runs over, the one named last changes fastest.
Arguments:
- elevation: float32 [2048, 1, 2, 128], P('gx', None, 'gy'), may hold values from -0.4 to 0.4
- velocity: float32 [2, 2048, 1, 2, 128], P(None, 'gx', None, 'gy'), may hold values from -2 to 2
- depth: float32 [2048, 1, 2, 128], P('gx', None, 'gy'), may hold values from 3 to 6
- turbine: float32 [2048, 1, 2, 128], P('gx', None, 'gy'), may hold values from 0.1 to 2
- wet_tiles: int32 [16, 1, 2], P('gx', None, 'gy'), may hold values 0 or 1
- farm: int32 [2048, 1, 2, 128], P('gx', None, 'gy'), may hold values from 0 to 31, as said below
Outputs:
- adjoint: float32 [3, 2048, 1, 2, 128], P(None, 'gx', None, 'gy')
- turbine_grad: float32 [2048, 1, 2, 128], P('gx', None, 'gy')
- farm_grad: float32 [32], P(('gx', 'gy'))
Inputs may be any that keep to these rules, and one draw needn't show every extreme that they name: A cell in tile row i, in a tile column of group j (its column modulo 2), belongs to farm i * 2 + j or to farm ((i + 1) mod 16) * 2 + j.
All inputs are finite; a program needn't handle non-finite values. No bound on the sum of `wet_tiles` on one device may be relied on, other than what follows from the above.
Results may differ from a plain program's by a relative error of at most 0.0002.
Values sent between devices are 32-bit elements; how exact they have to be, the bound alone decides.
No kernel may reach another device: no remote copies, remote signals or barrier semaphores. Data moves between devices by JAX's collectives and lax.ppermute only.
A program may use at most 64 MiB of HBM per device.

v0:
```python
import jax
import jax.numpy as jnp
from jax import lax
from jax.experimental import pallas as pl
from jax.experimental.pallas import tpu as pltpu
from jax.sharding import PartitionSpec as P

SPEED_EPS = 0.01
BED_DRAG = 0.1
LANES = 128
HALO = 24
GUARD = 8
OWN = GUARD + HALO
FIELDS = 5
STEP = 16
ADV = 0.1 / 12.0
GRAV = 0.3 / 12.0
VISC = 0.004


def pairings(count):
    even = [i ^ 1 for i in range(count)]
    if count == 2:
        return [even]
    odd = [i if i in (0, count - 1) else ((i + 1) ^ 1) - 1 for i in range(count)]
    return [even, odd]


def roles(axis, count):
    place = lax.axis_index(axis)
    odd = lax.rem(place, 2)
    after_a = 1 - odd
    result = [(after_a, True)]
    if count > 2:
        after_b = odd
        exists = jnp.where(after_b == 1, place < count - 1, place > 0)
        result.append((after_b, exists))
    return result


def pack_kernel(counts, wet_ref, elev_ref, vel_ref, depth_ref, turb_ref, *outs):
    rows = elev_ref.shape[0]
    fields = [elev_ref[...], vel_ref[0], vel_ref[1], depth_ref[...], turb_ref[...]]
    refs = [elev_ref, vel_ref.at[0], vel_ref.at[1], depth_ref, turb_ref]
    wet = wet_ref[0, 0, 0].astype(jnp.float32)
    roles_x = roles("gx", counts[0])
    roles_y = roles("gy", counts[1])
    outs = list(outs)
    row_outs = [outs.pop(0) for _ in roles_x]
    side_outs = [outs.pop(0) for _ in roles_y]
    starts = [pl.multiple_of(after * (rows - HALO), 8) for after, _ in roles_x]
    for start, out in zip(starts, row_outs):
        for f, ref in enumerate(refs):
            out[HALO * f : HALO * (f + 1), :] = ref[pl.ds(start, HALO), :]
        out[HALO * FIELDS :, :] = jnp.full((LANES - HALO * FIELDS, LANES), wet, jnp.float32)
    lane = lax.broadcasted_iota(jnp.int32, (rows, LANES), 1)
    for (after, _), out in zip(roles_y, side_outs):
        packed = jnp.full((rows, LANES), wet, jnp.float32)
        for f in reversed(range(FIELDS)):
            moved = jnp.where(
                after == 1,
                pltpu.roll(fields[f], HALO * (f + 1), 1),
                pltpu.roll(fields[f], HALO * f, 1),
            )
            packed = jnp.where(lane < HALO * (f + 1), moved, packed)
        out[...] = packed
    for start in starts:
        for side in side_outs:
            outs.pop(0)[...] = side[pl.ds(start, HALO), :]


def shift_y(field, by):
    return pltpu.roll(field, (-by) % LANES, 1)


def main_kernel(
    counts, wet_ref, elev_ref, vel_ref, depth_ref, turb_ref, farm_ref, *rest
):
    rows = elev_ref.shape[0]
    rest = list(rest)
    nx, ny = counts
    roles_x = roles("gx", nx)
    roles_y = roles("gy", ny)
    row_in = [rest.pop(0) for _ in roles_x]
    left_in = rest.pop(0)
    right_in = rest.pop(0)
    corner_in = [(rest.pop(0), rest.pop(0)) for _ in roles_x]
    adj_ref, grad_ref, own_sum_ref, other_sum_ref, S = rest
    place_x = lax.axis_index("gx")
    place_y = lax.axis_index("gy")
    has_left = place_y > 0
    has_right = place_y < ny - 1
    wet = wet_ref[0, 0, 0].astype(jnp.float32)

    names = ["w", "T", "c", "d"]
    for k in range(6):
        names += [n + str(k) for n in ("h", "u", "v", "H", "F", "xu", "xv", "yu", "yv", "dm", "E", "rH")]
        names += [n + str(k) for n in ("lh", "lu", "lv", "uu", "uv")]
    names += ["acc", "oh", "ou", "ov"]
    at = {n: i for i, n in enumerate(names)}

    def lane_of(n):
        return lax.broadcasted_iota(jnp.int32, (n, LANES), 1)

    def put(start, n, centre, left, right, wet_centre, exists):
        lane = lane_of(n)
        in_left = lane < HALO
        in_right = lane >= LANES - HALO

        def windows(f, value):
            c = centre(f)
            if exists is not True:
                c = jnp.where(exists, c, value)
            ok_left = has_left if exists is True else jnp.logical_and(has_left, exists)
            ok_right = has_right if exists is True else jnp.logical_and(has_right, exists)
            from_left = jnp.where(ok_left, pltpu.roll(left, (-HALO * f) % LANES, 1), value)
            from_right = jnp.where(ok_right, pltpu.roll(right, (-HALO * (f + 1)) % LANES, 1), value)
            return (
                jnp.where(in_left, from_left, pltpu.roll(c, HALO, 1)),
                jnp.where(in_right, from_right, pltpu.roll(c, LANES - HALO, 1)),
            )

        hs = windows(0, 0.0)
        us = windows(1, 0.0)
        vs = windows(2, 0.0)
        ds = windows(3, 1.0)
        ts = windows(4, 0.0)
        wc = wet_centre
        ok_left = has_left
        ok_right = has_right
        if exists is not True:
            wc = jnp.where(exists, wc, 0.0)
            ok_left = jnp.logical_and(has_left, exists)
            ok_right = jnp.logical_and(has_right, exists)
        wl = jnp.where(ok_left, jnp.broadcast_to(left[:, LANES - 1 :], (n, LANES)), 0.0)
        wr = jnp.where(ok_right, jnp.broadcast_to(right[:, LANES - 1 :], (n, LANES)), 0.0)
        ws = (jnp.where(in_left, wl, wc), jnp.where(in_right, wr, wc))
        for t in range(2):
            def store(name, value):
                S[at[name], t, pl.ds(start, n), :] = value

            store("w", ws[t])
            store("T", ts[t])
            store("c", 0.5 * (BED_DRAG + ts[t]))
            store("d", ds[t])
            store("h0", hs[t])
            store("u0", us[t])
            store("v0", vs[t])
            height = ds[t] + hs[t]
            store("H0", height)
            store("F0", height * us[t])

    own = [elev_ref, vel_ref.at[0], vel_ref.at[1], depth_ref, turb_ref]
    put(OWN, rows, lambda f: own[f][...], left_in[...], right_in[...], wet, True)
    for (after, exists), rin, (cl, cr) in zip(roles_x, row_in, corner_in):
        start = pl.multiple_of(GUARD + after * (rows + HALO), 8)
        put(
            start,
            HALO,
            lambda f: rin[HALO * f : HALO * (f + 1), :],
            cl[...],
            cr[...],
            jnp.broadcast_to(rin[LANES - 1 :, :], (HALO, LANES)),
            exists,
        )

    def sweep(blocks, body):
        def step(i, carry):
            r0 = pl.multiple_of(OWN - 8 * blocks + i * STEP, 8)
            for t in range(2):
                body(
                    lambda name, s=0: S[at[name], t, pl.ds(r0 + s, STEP), :],
                    lambda name, value: S.__setitem__((at[name], t, pl.ds(r0, STEP), slice(None)), value),
                )
            return carry

        lax.fori_loop(0, (rows + 16 * blocks) // STEP, step, 0)

    def d_rows(L, name):
        return 8.0 * (L(name, 1) - L(name, -1)) - (L(name, 2) - L(name, -2))

    def d_cols(f):
        e = f - shift_y(f, -2)
        return 8.0 * shift_y(e, 1) - (shift_y(e, 2) + e)

    def velocity_terms(L, name, f):
        up1, um1, up2, um2 = L(name, 1), L(name, -1), L(name, 2), L(name, -2)
        dx = 8.0 * (up1 - um1) - (up2 - um2)
        yp2, ym2 = shift_y(f, 2), shift_y(f, -2)
        dy = 8.0 * shift_y(f - ym2, 1) - (yp2 - ym2)
        g = (up1 + um1) - 4.0 * f
        sg = shift_y(g + shift_y(g, -2), 1)
        far = (up2 + um2) + (yp2 + ym2)
        bi = far - 12.0 * f + 2.0 * (sg - 4.0 * g)
        return dx, dy, bi

    def tend(L, St, k, with_h):
        u, v, H = L("u%d" % k), L("v%d" % k), L("H%d" % k)
        xu, yu, bu = velocity_terms(L, "u%d" % k, u)
        xv, yv, bv = velocity_terms(L, "v%d" % k, v)
        h = L("h%d" % k)
        xh = d_rows(L, "h%d" % k)
        yh = d_cols(h)
        q2 = u * u + v * v + SPEED_EPS
        rH = 1.0 / H
        E = L("c") * (lax.rsqrt(q2) * rH)
        damp = E * q2
        for name, value in (("xu", xu), ("xv", xv), ("yu", yu), ("yv", yv), ("dm", damp), ("E", E), ("rH", rH)):
            St(name + str(k), value)
        ku = -ADV * (u * xu + v * yu) - GRAV * xh - damp * u - VISC * bu
        kv = -ADV * (u * xv + v * yv) - GRAV * yh - damp * v - VISC * bv
        if not with_h:
            return None, ku, kv
        kh = -ADV * (d_rows(L, "F%d" % k) + d_cols(H * v))
        return kh, ku, kv

    def keep_state(L, St, k, h, u, v):
        H = L("d") + h
        St("h%d" % k, h)
        St("u%d" % k, u)
        St("v%d" % k, v)
        St("H%d" % k, H)
        St("F%d" % k, H * u)

    hb = [-(-(22 - 2 * k) // 8) for k in range(6)]
    for n in range(2):
        s, a, b = 3 * n, 3 * n + 1, 3 * n + 2

        def first(L, St):
            w = L("w")
            ks = tend(L, St, s, True)
            keep_state(L, St, a, *[w * (L(x + str(s)) + k) for x, k in zip("huv", ks)])

        sweep(hb[s], first)

        def second(L, St):
            w = L("w")
            ks = tend(L, St, a, True)
            keep_state(
                L, St, b,
                *[w * (0.75 * L(x + str(s)) + 0.25 * (L(x + str(a)) + k)) for x, k in zip("huv", ks)],
            )

        sweep(hb[a], second)

        def third(L, St):
            w = L("w")
            ks = tend(L, St, b, n == 0)
            new = [
                None if k is None else w * (L(x + str(s)) * (1.0 / 3.0) + (2.0 / 3.0) * (L(x + str(b)) + k))
                for x, k in zip("huv", ks)
            ]
            if n == 0:
                keep_state(L, St, 3, *new)
                return
            u, v = new[1], new[2]
            q2 = u * u + v * v + SPEED_EPS
            q = jnp.sqrt(q2)
            St("acc", w * q2 * q)
            fac = (2.0 * w) * (L("T") * w * q)
            lu, lv = fac * u, fac * v
            ub = L("u5")
            St("lu5", lu)
            St("lv5", lv)
            St("uu5", ub * lu)
            St("uv5", ub * lv)

        sweep(hb[b], third)

    def pull(L, St, k, with_h):
        u, v, H = L("u%d" % k), L("v%d" % k), L("H%d" % k)
        lu, lv = L("lu%d" % k), L("lv%d" % k)
        nlu, nlv = "lu%d" % k, "lv%d" % k
        damp, E, rH = L("dm%d" % k), L("E%d" % k), L("rH%d" % k)
        xlu, _, blu = velocity_terms(L, nlu, lu)
        _, ylv, blv = velocity_terms(L, nlv, lv)
        r = lu * u + lv * v
        rd = r * damp
        rE = r * E
        ub = d_rows(L, "uu%d" % k) + d_cols(v * lu) - lu * L("xu%d" % k) - lv * L("xv%d" % k)
        vb = d_rows(L, "uv%d" % k) + d_cols(v * lv) - lu * L("yu%d" % k) - lv * L("yv%d" % k)
        hbar = GRAV * (xlu + ylv) + rd * rH
        if with_h:
            xlh = d_rows(L, "lh%d" % k)
            ylh = d_cols(L("lh%d" % k))
            ub = ub + H * xlh
            vb = vb + H * ylh
            hbar = hbar + ADV * (u * xlh + v * ylh)
        ub = ADV * ub - VISC * blu - (damp * lu + rE * u)
        vb = ADV * vb - VISC * blv - (damp * lv + rE * v)
        return hbar, ub, vb, rd

    drag = {k: [] for k in range(6)}

    def cot(L, name, k):
        return L(name + str(k))

    def keep_cot(L, St, k, lh, lu, lv):
        u = L("u%d" % k)
        St("lh%d" % k, lh)
        St("lu%d" % k, lu)
        St("lv%d" % k, lv)
        St("uu%d" % k, u * lu)
        St("uv%d" % k, u * lv)

    bb = [-(-(10 - 2 * k) // 8) for k in range(6)]
    for n in (1, 0):
        s, a, b = 3 * n, 3 * n + 1, 3 * n + 2
        first_pull = n == 1

        def from_b(L, St):
            w = L("w")
            hbar, ub, vb, rd = pull(L, St, b, not first_pull)
            St("acc", L("acc") - rd / (2.0 * L("c")))
            nh = hbar if first_pull else hbar + cot(L, "lh", b)
            quarter = 0.25 * w
            keep_cot(L, St, a, quarter * nh, quarter * (ub + cot(L, "lu", b)), quarter * (vb + cot(L, "lv", b)))

        sweep(bb[5 - b], from_b)

        def from_a(L, St):
            w = L("w")
            hbar, ub, vb, rd = pull(L, St, a, True)
            St("acc", L("acc") - rd / (2.0 * L("c")))
            keep_cot(
                L, St, s,
                w * (hbar + cot(L, "lh", a)), w * (ub + cot(L, "lu", a)), w * (vb + cot(L, "lv", a)),
            )

        sweep(bb[5 - a], from_a)

        def from_s(L, St):
            w = L("w")
            hbar, ub, vb, rd = pull(L, St, s, True)
            St("acc", L("acc") - rd / (2.0 * L("c")))
            new = []
            for x, value in (("lh", hbar), ("lu", ub), ("lv", vb)):
                total = value + cot(L, x, s) + 3.0 * cot(L, x, a)
                if not (first_pull and x == "lh"):
                    total = total + 0.5 * cot(L, x, b)
                new.append(total)
            if first_pull:
                scale = (2.0 / 3.0) * w
                keep_cot(L, St, 2, *[scale * x for x in new])
            else:
                for name, value in zip(("oh", "ou", "ov"), new):
                    St(name, value)

        sweep(bb[5 - s], from_s)

    def own_columns(name):
        lane = lane_of(rows)
        return jnp.where(
            lane < LANES // 2,
            pltpu.roll(S[at[name], 0, OWN : OWN + rows, :], LANES - HALO, 1),
            pltpu.roll(S[at[name], 1, OWN : OWN + rows, :], HALO, 1),
        )

    for i, name in enumerate(("oh", "ou", "ov")):
        adj_ref[i] = own_columns(name)
    grad = own_columns("acc")
    grad_ref[...] = grad
    matched = farm_ref[...] == place_x * ny + place_y
    scale = 1.0 / (rows * LANES)
    own_sum_ref[0] = jnp.sum(jnp.where(matched, grad, 0.0)) * scale
    other_sum_ref[0] = jnp.sum(jnp.where(matched, 0.0, grad)) * scale


def shards(elevation, velocity, depth, turbine, wet_tiles, farm):
    rows = elevation.shape[0]
    counts = (lax.axis_size("gx"), lax.axis_size("gy"))
    nx, ny = counts
    elev = elevation.reshape(rows, LANES)
    vel = velocity.reshape(2, rows, LANES)
    dep = depth.reshape(rows, LANES)
    turb = turbine.reshape(rows, LANES)
    farm_local = farm.reshape(rows, LANES)
    pairs_x = pairings(nx)
    pairs_y = pairings(ny)
    f32 = jnp.float32
    square = jax.ShapeDtypeStruct((LANES, LANES), f32)
    side = jax.ShapeDtypeStruct((rows, LANES), f32)
    corner = jax.ShapeDtypeStruct((HALO, LANES), f32)
    vmem = pl.BlockSpec(memory_space=pltpu.VMEM)
    smem = pl.BlockSpec(memory_space=pltpu.SMEM)
    shapes = [square] * len(pairs_x) + [side] * len(pairs_y) + [corner] * (len(pairs_x) * len(pairs_y))
    sent = pl.pallas_call(
        lambda *refs: pack_kernel(counts, *refs),
        out_shape=shapes,
        in_specs=[smem] + [vmem] * 4,
        out_specs=[vmem] * len(shapes),
        name="pack",
    )(wet_tiles, elev, vel, dep, turb)
    sent = list(sent)
    row_got = [lax.ppermute(sent.pop(0), "gx", list(enumerate(p))) for p in pairs_x]
    side_got = [lax.ppermute(sent.pop(0), "gy", list(enumerate(p))) for p in pairs_y]
    corner_got = [
        [
            lax.ppermute(
                sent.pop(0),
                ("gx", "gy"),
                [(i * ny + j, px[i] * ny + py[j]) for i in range(nx) for j in range(ny)],
            )
            for py in pairs_y
        ]
        for px in pairs_x
    ]

    def left_right(got):
        if len(got) == 1:
            return got[0], got[0]
        odd = lax.rem(lax.axis_index("gy"), 2) == 1
        return jnp.where(odd, got[0], got[1]), jnp.where(odd, got[1], got[0])

    left, right = left_right(side_got)
    corners = [c for got in corner_got for c in left_right(got)]
    n_in = 6 + len(row_got) + 2 + len(corners)
    planes = 4 + 6 * 17 + 4
    adjoint, grad, own_sum, other_sum = pl.pallas_call(
        lambda *refs: main_kernel(counts, *refs),
        out_shape=[
            jax.ShapeDtypeStruct((3, rows, LANES), f32),
            side,
            jax.ShapeDtypeStruct((1,), f32),
            jax.ShapeDtypeStruct((1,), f32),
        ],
        in_specs=[smem] + [vmem] * (n_in - 1),
        out_specs=[vmem, vmem, smem, smem],
        scratch_shapes=[pltpu.VMEM((planes, 2, rows + 2 * OWN, LANES), f32)],
        compiler_params=pltpu.CompilerParams(vmem_limit_bytes=40 * 1024 * 1024),
        name="adjoint",
    )(wet_tiles, elev, vel, dep, turb, farm_local, *row_got, left, right, *corners)
    passed = lax.ppermute(other_sum, "gx", [(i, (i + 1) % nx) for i in range(nx)])
    return (
        adjoint.reshape((3,) + elevation.shape),
        grad.reshape(elevation.shape),
        own_sum + passed,
    )


def solution(mesh):
    in_specs = (
        P("gx", None, "gy", None),
        P(None, "gx", None, "gy", None),
        P("gx", None, "gy", None),
        P("gx", None, "gy", None),
        P("gx", None, "gy"),
        P("gx", None, "gy", None),
    )
    out_specs = (P(None, "gx", None, "gy", None), P("gx", None, "gy", None), P(("gx", "gy")))
    return jax.shard_map(shards, mesh=mesh, in_specs=in_specs, out_specs=out_specs, check_vma=False)
```

profile of v0, /device:TPU:0, one launch (start us, length us, event | category | flops | bytes accessed | tf_op | source)
XLA Modules:
  0.0 46.4 jit_solution(6756317410228969387)
XLA Ops:
  1.3 0.0 copy-start
  1.3 0.0 copy-start.1
  1.3 0.0 copy-start.2
  1.3 0.0 copy-start.3
  1.3 1.9 %pack.1 = (f32[128,128]{1,0:T(8,128)}, f32[128,128]{1,0:T(8,128)}, f32[128,128]{1,0:T(8,128)}, f32[24,128]{1,0:T(8,128)}, f32[24,128]{1,0:T(8,128)}) custom-call(s32[1,1,1]{2,1,0:T(1,128)S(6)} %copy.11.refs_0_, f32[128,128]{1,0:T(8,128)} %bitcast.13, f32[2,128,128]{2,1,0:T(8,128)} %bitcast.11, f32[128,128]{1,0:T(8,128)} %bitcast.15, f32[128,128]{1,0:T(8,128)} %bitcast.17), custom_call_target="tpu_custom_call" | custom-call | tf_op jit(solution)/shard_map/pack/pallas_call | solution.py:387
  3.2 0.5 collective-permute-start
  3.7 1.5 %collective-permute-start.1 = (f32[128,128]{1,0:T(8,128)}, f32[128,128]{1,0:T(8,128)S(1)}, u32[]{:S(2)}, u32[]{:S(2)}) collective-permute-start(f32[128,128]{1,0:T(8,128)} %get-tuple-element.13), channel_id=1, source_target_pairs={{0,0},{2,4},{4,2},{6,8},{8,6},{10,12},{12,10},{14,16},{16,14},{18,... | collective-permute-start | bytes 196616 | tf_op jit(solution)/shard_map/ppermute | solution.py:395
  5.1 2.5 %collective-permute-start.2 = (f32[128,128]{1,0:T(8,128)}, f32[128,128]{1,0:T(8,128)S(1)}, u32[]{:S(2)}, u32[]{:S(2)}) collective-permute-start(f32[128,128]{1,0:T(8,128)} %get-tuple-element.14), channel_id=1, source_target_pairs={{0,1},{1,0},{2,3},{3,2},{4,5},{5,4},{6,7},{7,6},{8,9},{9,8},{10,11... | collective-permute-start | bytes 196616 | tf_op jit(solution)/shard_map/ppermute | solution.py:396
  7.7 1.9 %collective-permute-start.3 = (f32[24,128]{1,0:T(8,128)}, f32[24,128]{1,0:T(8,128)S(1)}, u32[]{:S(2)}, u32[]{:S(2)}) collective-permute-start(f32[24,128]{1,0:T(8,128)} %get-tuple-element.15), channel_id=1, source_target_pairs={{0,3},{1,2},{2,1},{3,0},{4,7},{5,6},{6,5},{7,4},{8,11},{9,10},{10,... | collective-permute-start | bytes 36872 | tf_op jit(solution)/shard_map/ppermute | solution.py:399
  9.6 1.5 %collective-permute-start.4 = (f32[24,128]{1,0:T(8,128)}, f32[24,128]{1,0:T(8,128)S(1)}, u32[]{:S(2)}, u32[]{:S(2)}) collective-permute-start(f32[24,128]{1,0:T(8,128)} %get-tuple-element.16), channel_id=1, source_target_pairs={{0,1},{1,0},{2,5},{3,4},{4,3},{5,2},{6,9},{7,8},{8,7},{9,6},{10,13... | collective-permute-start | bytes 36872 | tf_op jit(solution)/shard_map/ppermute | solution.py:399
  11.1 0.8 %collective-permute-done.3.refs_10_.refs_11_ = f32[24,128]{1,0:T(8,128)S(1)} collective-permute-done((f32[24,128]{1,0:T(8,128)}, f32[24,128]{1,0:T(8,128)S(1)}, u32[]{:S(2)}, u32[]{:S(2)}) %collective-permute-start.3) | collective-permute-done | bytes 12320 | tf_op jit(solution)/shard_map/ppermute | solution.py:399
  11.9 1.6 %collective-permute-done.4.refs_12_.refs_13_ = f32[24,128]{1,0:T(8,128)S(1)} collective-permute-done((f32[24,128]{1,0:T(8,128)}, f32[24,128]{1,0:T(8,128)S(1)}, u32[]{:S(2)}, u32[]{:S(2)}) %collective-permute-start.4) | collective-permute-done | bytes 12320 | tf_op jit(solution)/shard_map/ppermute | solution.py:399
  13.5 0.0 collective-permute-done.refs_6_
  13.5 0.0 collective-permute-done.1.refs_7_
  13.5 0.0 collective-permute-done.2.refs_8_.refs_9_
  13.5 0.0 copy-done
  13.5 0.0 copy-done.1
  13.5 0.0 copy-done.2
  13.5 0.0 copy-done.3
  13.5 0.0 copy-start.4
  13.6 0.8 %copy-done.4 = s32[128,1,1,128]{3,2,1,0:T(1,128)S(1)} copy-done((s32[128,1,1,128]{3,2,1,0:T(1,128)S(1)}, s32[128,1,1,128]{3,2,1,0:T(1,128)}, u32[]{:S(2)}) %copy-start.4) | copy-done | bytes 65560
  14.4 23.8 %adjoint.1 = (f32[3,128,128]{2,1,0:T(8,128)}, f32[128,128]{1,0:T(8,128)}, f32[1]{0:T(128)}, f32[1]{0:T(128)}) custom-call(s32[1,1,1]{2,1,0:T(1,128)S(6)} %copy.11.refs_0_, f32[128,128]{1,0:T(8,128)S(1)} %bitcast.14, f32[2,128,128]{2,1,0:T(8,128)S(1)} %bitcast.12, f32[128,128]{1,0:T(8,128)S(1)} %bitcast.16, f32[128,128]{1,0:T(8,128)S(1)} %bitcast.18, ...), custom_call_target="tpu_custom_call" | custom-call | tf_op jit(solution)/shard_map/adjoint/pallas_call | solution.py:419
  38.2 0.4 collective-permute-start.5
  38.5 5.5 %collective-permute-done.5 = f32[1]{0:T(128)} collective-permute-done((f32[1]{0:T(128)}, f32[1]{0:T(128)}, u32[]{:S(2)}, u32[]{:S(2)}) %collective-permute-start.5) | collective-permute-done | bytes 36 | tf_op jit(solution)/shard_map/ppermute | solution.py:433
Async XLA Ops:
  1.3 12.2 %copy-start = (f32[2,128,1,1,128]{4,3,2,1,0:T(1,128)S(1)}, f32[2,128,1,1,128]{4,3,2,1,0:T(1,128)}, u32[]{:S(2)}) copy-start(f32[2,128,1,1,128]{4,3,2,1,0:T(1,128)} %param.7) | copy-start | bytes 393220
  1.3 12.2 %copy-start.1 = (f32[128,1,1,128]{3,2,1,0:T(1,128)S(1)}, f32[128,1,1,128]{3,2,1,0:T(1,128)}, u32[]{:S(2)}) copy-start(f32[128,1,1,128]{3,2,1,0:T(1,128)} %param.6) | copy-start | bytes 196612
  1.3 12.2 %copy-start.2 = (f32[128,1,1,128]{3,2,1,0:T(1,128)S(1)}, f32[128,1,1,128]{3,2,1,0:T(1,128)}, u32[]{:S(2)}) copy-start(f32[128,1,1,128]{3,2,1,0:T(1,128)} %param.8) | copy-start | bytes 196612
  1.3 12.2 %copy-start.3 = (f32[128,1,1,128]{3,2,1,0:T(1,128)S(1)}, f32[128,1,1,128]{3,2,1,0:T(1,128)}, u32[]{:S(2)}) copy-start(f32[128,1,1,128]{3,2,1,0:T(1,128)} %param.9) | copy-start | bytes 196612
  3.2 10.3 %collective-permute-start = (f32[128,128]{1,0:T(8,128)}, f32[128,128]{1,0:T(8,128)S(1)}, u32[]{:S(2)}, u32[]{:S(2)}) collective-permute-start(f32[128,128]{1,0:T(8,128)} %get-tuple-element.12), channel_id=1, source_target_pairs={{0,2},{2,0},{4,6},{6,4},{8,10},{10,8},{12,14},{14,12},{16,18},{18,... | collective-permute-start | bytes 196616 | tf_op jit(solution)/shard_map/ppermute | solution.py:395
  3.7 9.8 %collective-permute-start.1 = (f32[128,128]{1,0:T(8,128)}, f32[128,128]{1,0:T(8,128)S(1)}, u32[]{:S(2)}, u32[]{:S(2)}) collective-permute-start(f32[128,128]{1,0:T(8,128)} %get-tuple-element.13), channel_id=1, source_target_pairs={{0,0},{2,4},{4,2},{6,8},{8,6},{10,12},{12,10},{14,16},{16,14},{18,... | collective-permute-start | bytes 196616 | tf_op jit(solution)/shard_map/ppermute | solution.py:395
  5.1 8.4 %collective-permute-start.2 = (f32[128,128]{1,0:T(8,128)}, f32[128,128]{1,0:T(8,128)S(1)}, u32[]{:S(2)}, u32[]{:S(2)}) collective-permute-start(f32[128,128]{1,0:T(8,128)} %get-tuple-element.14), channel_id=1, source_target_pairs={{0,1},{1,0},{2,3},{3,2},{4,5},{5,4},{6,7},{7,6},{8,9},{9,8},{10,11... | collective-permute-start | bytes 196616 | tf_op jit(solution)/shard_map/ppermute | solution.py:396
  7.7 4.2 %collective-permute-start.3 = (f32[24,128]{1,0:T(8,128)}, f32[24,128]{1,0:T(8,128)S(1)}, u32[]{:S(2)}, u32[]{:S(2)}) collective-permute-start(f32[24,128]{1,0:T(8,128)} %get-tuple-element.15), channel_id=1, source_target_pairs={{0,3},{1,2},{2,1},{3,0},{4,7},{5,6},{6,5},{7,4},{8,11},{9,10},{10,... | collective-permute-start | bytes 36872 | tf_op jit(solution)/shard_map/ppermute | solution.py:399
  9.6 3.9 %collective-permute-start.4 = (f32[24,128]{1,0:T(8,128)}, f32[24,128]{1,0:T(8,128)S(1)}, u32[]{:S(2)}, u32[]{:S(2)}) collective-permute-start(f32[24,128]{1,0:T(8,128)} %get-tuple-element.16), channel_id=1, source_target_pairs={{0,1},{1,0},{2,5},{3,4},{4,3},{5,2},{6,9},{7,8},{8,7},{9,6},{10,13... | collective-permute-start | bytes 36872 | tf_op jit(solution)/shard_map/ppermute | solution.py:399
  13.5 0.8 %copy-start.4 = (s32[128,1,1,128]{3,2,1,0:T(1,128)S(1)}, s32[128,1,1,128]{3,2,1,0:T(1,128)}, u32[]{:S(2)}) copy-start(s32[128,1,1,128]{3,2,1,0:T(1,128)} %param.11) | copy-start | bytes 196612
  38.2 5.9 %collective-permute-start.5 = (f32[1]{0:T(128)}, f32[1]{0:T(128)}, u32[]{:S(2)}, u32[]{:S(2)}) collective-permute-start(f32[1]{0:T(128)} %get-tuple-element.20), channel_id=1, source_target_pairs={{0,2},{2,4},{4,6},{6,8},{8,10},{10,12},{12,14},{14,16},{16,18},{18... | collective-permute-start | bytes 20 | tf_op jit(solution)/shard_map/ppermute | solution.py:433
where the time goes:
time: 46.7 us; the launch traced here: 46.4 us
  Pallas kernels  25.7 us (55%)
  starting transfers between devices  8.25 us (18%)
  waiting for transfers between devices  7.92 us (17%)
  between operations  3.7 us (8%)
  local copies, waits for them, and re-layouts  0.85 us (2%)
    pallas_call x1, Pallas kernels, shards(): pl.pallas_call(lambda *refs: main_kernel(counts, *refs), out_shape=[jax.S...  23.8 us
    ppermute x1, waiting for transfers between devices, shards(): lax.ppermute(other_sum, 'gx', [(i, (i + 1) % nx) for i in range(nx)])  5.52 us
    ppermute x2, starting transfers between devices, shards(): lax.ppermute(sent.pop(0), ('gx', 'gy'), [(i * ny + j, px[i] * ny + py[j])...  3.44 us
    ppermute x1, starting transfers between devices, shards(): lax.ppermute(sent.pop(0), 'gy', list(enumerate(p)))  2.52 us
    ppermute x2, waiting for transfers between devices, shards(): lax.ppermute(sent.pop(0), ('gx', 'gy'), [(i * ny + j, px[i] * ny + py[j])...  2.39 us
    ppermute x2, starting transfers between devices, shards(): lax.ppermute(sent.pop(0), 'gx', list(enumerate(p)))  1.94 us
    pallas_call x1, Pallas kernels, shards(): pl.pallas_call(lambda *refs: pack_kernel(counts, *refs), out_shape=shapes...  1.88 us
  transfers between devices with their start and end apart: 6, of which 3 were waited for; matrix products, arithmetic and copies ran while one was open for 0% of the time, Pallas kernels for 0%

commit v1 on v0

v1 whole, which is shorter than its diff:
```python
import jax
import jax.numpy as jnp
from jax import lax
from jax.experimental import pallas as pl
from jax.experimental.pallas import tpu as pltpu
from jax.sharding import PartitionSpec as P

SPEED_EPS = 0.01
BED_DRAG = 0.1
LANES = 128
HALO = 24
GUARD = 8
OWN = GUARD + HALO
FIELDS = 5
STEP = 16
UNROLL = 2
WIDE = LANES + 2 * HALO
ADV = 0.1 / 12.0
GRAV = 0.3 / 12.0
VISC = 0.004


def pairings(count):
    even = [i ^ 1 for i in range(count)]
    if count == 2:
        return [even]
    odd = [i if i in (0, count - 1) else ((i + 1) ^ 1) - 1 for i in range(count)]
    return [even, odd]


def roles(axis, count):
    place = lax.axis_index(axis)
    odd = lax.rem(place, 2)
    after_a = 1 - odd
    result = [(after_a, True)]
    if count > 2:
        after_b = odd
        exists = jnp.where(after_b == 1, place < count - 1, place > 0)
        result.append((after_b, exists))
    return result


def pack_kernel(counts, wet_ref, elev_ref, vel_ref, depth_ref, turb_ref, *outs):
    rows = elev_ref.shape[0]
    fields = [elev_ref[...], vel_ref[0], vel_ref[1], depth_ref[...], turb_ref[...]]
    refs = [elev_ref, vel_ref.at[0], vel_ref.at[1], depth_ref, turb_ref]
    wet = wet_ref[...].astype(jnp.float32)
    roles_x = roles("gx", counts[0])
    roles_y = roles("gy", counts[1])
    outs = list(outs)
    row_outs = [outs.pop(0) for _ in roles_x]
    side_outs = [outs.pop(0) for _ in roles_y]
    starts = [pl.multiple_of(after * (rows - HALO), 8) for after, _ in roles_x]
    for start, out in zip(starts, row_outs):
        for f, ref in enumerate(refs):
            out[HALO * f : HALO * (f + 1), :] = ref[pl.ds(start, HALO), :]
        out[HALO * FIELDS :, :] = jnp.broadcast_to(wet, (LANES - HALO * FIELDS, LANES))
    lane = lax.broadcasted_iota(jnp.int32, (rows, LANES), 1)
    for (after, _), out in zip(roles_y, side_outs):
        packed = jnp.broadcast_to(wet, (rows, LANES))
        for f in reversed(range(FIELDS)):
            moved = jnp.where(
                after == 1,
                pltpu.roll(fields[f], HALO * (f + 1), 1),
                pltpu.roll(fields[f], HALO * f, 1),
            )
            packed = jnp.where(lane < HALO * (f + 1), moved, packed)
        out[...] = packed
    for start in starts:
        for side in side_outs:
            outs.pop(0)[...] = side[pl.ds(start, HALO), :]


class Pair:
    def __init__(self, even, odd):
        self.even, self.odd = even, odd

    def map(self, function):
        return Pair(function(self.even), function(self.odd))

    def __add__(self, other):
        return both(self, other, lambda a, b: a + b)

    def __sub__(self, other):
        return both(self, other, lambda a, b: a - b)

    def __mul__(self, other):
        return both(self, other, lambda a, b: a * b)

    def __truediv__(self, other):
        return both(self, other, lambda a, b: a / b)

    def __rmul__(self, other):
        return self.map(lambda a: other * a)


def both(a, b, function):
    if isinstance(b, Pair):
        return Pair(function(a.even, b.even), function(a.odd, b.odd))
    return Pair(function(a.even, b), function(a.odd, b))


def after(x):
    return pltpu.roll(x, LANES - 1, 1)


def before(x):
    return pltpu.roll(x, 1, 1)


def d_cols(f):
    ea, eb, oa, ob = after(f.even), before(f.even), after(f.odd), before(f.odd)
    slope = Pair(
        8.0 * (f.odd - ob) - (ea - eb),
        8.0 * (ea - f.even) - (oa - ob),
    )
    return slope, Pair(ea + eb, oa + ob)


def combine(p1, m1, p2, m2):
    return Pair(
        (p1.odd + after(p2.even)) + before(m1.odd + m2.even),
        (m1.even + after(p1.even + p2.odd)) + before(m2.odd),
    )


def thirds(x):
    one = x.astype(jnp.bfloat16)
    rest = x - one.astype(jnp.float32)
    two = rest.astype(jnp.bfloat16)
    three = (rest - two.astype(jnp.float32)).astype(jnp.bfloat16)
    return one, two, three


def pick(x, chosen):
    parts = [jnp.dot(part, chosen, preferred_element_type=jnp.float32) for part in thirds(x)]
    return (parts[0] + parts[1]) + parts[2]


def main_kernel(counts, wet_ref, elev_ref, vel_ref, depth_ref, turb_ref, farm_ref, *rest):
    rows = elev_ref.shape[0]
    rest = list(rest)
    nx, ny = counts
    roles_x = roles("gx", nx)
    row_in = [rest.pop(0) for _ in roles_x]
    sides = 1 if ny == 2 else 2
    side_in = [rest.pop(0) for _ in range(sides)]
    corner_in = [[rest.pop(0) for _ in range(sides)] for _ in roles_x]
    adj_ref, grad_ref, own_sum_ref, other_sum_ref, S = rest
    place_x = lax.axis_index("gx")
    place_y = lax.axis_index("gy")
    has_left = place_y > 0
    has_right = place_y < ny - 1
    wet = wet_ref[...].astype(jnp.float32)

    names = ["w", "T", "c", "d"]
    for k in range(6):
        names += [n + str(k) for n in ("h", "u", "v", "H", "F", "xu", "xv", "yu", "yv", "dm", "E", "rH")]
        names += [n + str(k) for n in ("lh", "lu", "lv", "uu", "uv")]
    names += ["acc", "oh", "ou", "ov"]
    at = {n: i for i, n in enumerate(names)}

    def column_at(shape, dim):
        place = lax.broadcasted_iota(jnp.int32, shape, dim)
        return 2 * lax.rem(place, LANES) + lax.div(place, LANES)

    def spread(f):
        shape = (LANES, 2 * LANES)
        target = column_at(shape, 1)
        source = lax.broadcasted_iota(jnp.int32, shape, 0)
        blocks = [source + HALO == target]
        edge = source - HALO * f
        inside = jnp.logical_and(edge >= 0, edge < HALO)
        if sides == 1:
            offset = jnp.where(has_left, 0, LANES + HALO)
            blocks.append(jnp.logical_and(inside, edge + offset == target))
        else:
            hit_left = jnp.logical_and(inside, edge == target)
            hit_right = jnp.logical_and(inside, edge + (LANES + HALO) == target)
            blocks.append(jnp.logical_and(hit_left, has_left))
            blocks.append(jnp.logical_and(hit_right, has_right))
        return jnp.concatenate(
            [jnp.where(b, 1.0, 0.0).astype(jnp.bfloat16) for b in blocks], axis=0
        )

    chosen = [spread(f) for f in range(FIELDS)]

    def put(start, n, centre, edges, wet_centre, exists):
        column = column_at((n, 2 * LANES), 1)
        in_left = column < HALO
        in_right = column >= LANES + HALO
        known = jnp.logical_and(
            jnp.logical_or(jnp.logical_not(in_left), has_left),
            jnp.logical_or(jnp.logical_not(in_right), has_right),
        )
        known = jnp.logical_and(known, column < WIDE)
        if exists is not True:
            known = jnp.logical_and(known, exists)
        values = [
            jnp.where(known, pick(jnp.concatenate([centre(f)] + edges, axis=1), chosen[f]), 1.0 if f == 3 else 0.0)
            for f in range(FIELDS)
        ]
        wet_left = jnp.broadcast_to(edges[0][:, LANES - 1 :], (n, 2 * LANES))
        wet_right = jnp.broadcast_to(edges[-1][:, LANES - 1 :], (n, 2 * LANES))
        w = jnp.where(in_left, wet_left, jnp.where(in_right, wet_right, wet_centre))
        w = jnp.where(known, w, 0.0)
        h, u, v, d, turb = values
        height = d + h
        planes = (
            ("w", w), ("T", turb), ("c", 0.5 * (BED_DRAG + turb)), ("d", d),
            ("h0", h), ("u0", u), ("v0", v), ("H0", height), ("F0", height * u),
        )
        for name, value in planes:
            for t in range(2):
                S[at[name], t, pl.ds(start, n), :] = value[:, LANES * t : LANES * (t + 1)]

    own = [elev_ref, vel_ref.at[0], vel_ref.at[1], depth_ref, turb_ref]
    put(
        OWN, rows, lambda f: own[f][...], [x[...] for x in side_in],
        jnp.broadcast_to(wet, (rows, 2 * LANES)), True,
    )
    for (partner_after, exists), rin, corners in zip(roles_x, row_in, corner_in):
        put(
            pl.multiple_of(GUARD + partner_after * (rows + HALO), 8),
            HALO,
            lambda f: rin[HALO * f : HALO * (f + 1), :],
            [x[...] for x in corners],
            jnp.broadcast_to(rin[LANES - 1 :, :1], (HALO, 2 * LANES)),
            exists,
        )

    def sweep(blocks, body):
        count = (rows + 16 * blocks) // STEP

        def chunk(r0):
            def load(name, s=0):
                return Pair(*[S[at[name], t, pl.ds(r0 + s, STEP), :] for t in range(2)])

            def store(name, value):
                S[at[name], 0, pl.ds(r0, STEP), :] = value.even
                S[at[name], 1, pl.ds(r0, STEP), :] = value.odd

            body(load, store)

        def step(i, carry):
            for k in range(UNROLL):
                chunk(pl.multiple_of(OWN - 8 * blocks + (i * UNROLL + k) * STEP, 8))
            return carry

        lax.fori_loop(0, count // UNROLL, step, 0)
        for k in range(count // UNROLL * UNROLL, count):
            chunk(OWN - 8 * blocks + k * STEP)

    def d_rows(L, name):
        p1, m1, p2, m2 = L(name, 1), L(name, -1), L(name, 2), L(name, -2)
        return 8.0 * (p1 - m1) - (p2 - m2), p1 + m1, p2 + m2

    def tend(L, St, k, with_h):
        u, v, H, h = L("u%d" % k), L("v%d" % k), L("H%d" % k), L("h%d" % k)
        xu, su, tu = d_rows(L, "u%d" % k)
        xv, sv, tv = d_rows(L, "v%d" % k)
        yu, ru = d_cols(u)
        yv, rv = d_cols(v)
        gu = su - 4.0 * u
        gv = sv - 4.0 * v
        near_u = Pair(gu.odd + before(gu.odd), gu.even + after(gu.even))
        bu = ((tu + ru) - 12.0 * u) + 2.0 * (near_u - 4.0 * gu)
        bv = ((tv + rv) - 12.0 * v) - 8.0 * gv
        far = 8.0 * h
        near_v = (2.0 * VISC / GRAV) * gv
        yh = combine(far + near_v, near_v - far, -1.0 * h, h)
        xh = d_rows(L, "h%d" % k)[0]
        q2 = (u * u + v * v) + SPEED_EPS
        rH = H.map(lambda x: 1.0 / x)
        E = L("c") * (q2.map(lax.rsqrt) * rH)
        damp = E * q2
        for name, value in (("xu", xu), ("xv", xv), ("yu", yu), ("yv", yv), ("dm", damp), ("E", E), ("rH", rH)):
            St(name + str(k), value)
        ku = (-ADV) * (u * xu + v * yu) - GRAV * xh - damp * u - VISC * bu
        kv = (-ADV) * (u * xv + v * yv) - GRAV * yh - damp * v - VISC * bv
        if not with_h:
            return None, ku, kv
        kh = (-ADV) * (d_rows(L, "F%d" % k)[0] + d_cols(H * v)[0])
        return kh, ku, kv

    def keep_state(L, St, k, h, u, v):
        H = L("d") + h
        St("h%d" % k, h)
        St("u%d" % k, u)
        St("v%d" % k, v)
        St("H%d" % k, H)
        St("F%d" % k, H * u)

    hb = [-(-(22 - 2 * k) // 8) for k in range(6)]
    for n in range(2):
        s, a, b = 3 * n, 3 * n + 1, 3 * n + 2

        def first(L, St):
            w = L("w")
            ks = tend(L, St, s, True)
            keep_state(L, St, a, *[w * (L(x + str(s)) + k) for x, k in zip("huv", ks)])

        sweep(hb[s], first)

        def second(L, St):
            w = L("w")
            ks = tend(L, St, a, True)
            keep_state(
                L, St, b,
                *[w * (0.75 * L(x + str(s)) + 0.25 * (L(x + str(a)) + k)) for x, k in zip("huv", ks)],
            )

        sweep(hb[a], second)

        def third(L, St):
            w = L("w")
            ks = tend(L, St, b, n == 0)
            new = [
                None if k is None else w * ((1.0 / 3.0) * L(x + str(s)) + (2.0 / 3.0) * (L(x + str(b)) + k))
                for x, k in zip("huv", ks)
            ]
            if n == 0:
                keep_state(L, St, 3, *new)
                return
            u, v = new[1], new[2]
            q2 = (u * u + v * v) + SPEED_EPS
            q = q2.map(jnp.sqrt)
            St("acc", w * q2 * q)
            fac = (2.0 * w) * (L("T") * w * q)
            lu, lv = fac * u, fac * v
            ub = L("u5")
            St("lu5", lu)
            St("lv5", lv)
            St("uu5", ub * lu)
            St("uv5", ub * lv)

        sweep(hb[b], third)

    def pull(L, k, with_h):
        u, v, H = L("u%d" % k), L("v%d" % k), L("H%d" % k)
        lu, lv = L("lu%d" % k), L("lv%d" % k)
        damp, E, rH = L("dm%d" % k), L("E%d" % k), L("rH%d" % k)
        visc = VISC / ADV
        xlu, su, tu = d_rows(L, "lu%d" % k)
        _, sv, tv = d_rows(L, "lv%d" % k)
        ylv, rv = d_cols(lv)
        gu = su - 4.0 * lu
        gv = sv - 4.0 * lv
        vl = v * lu
        vl8, near, lu_s = 8.0 * vl, (2.0 * visc) * gu, visc * lu
        ub = combine(vl8 - near, -1.0 * (vl8 + near), -1.0 * (vl + lu_s), vl - lu_s)
        ub = ub - visc * ((tu - 12.0 * lu) - 8.0 * gu)
        vl = v * lv
        vl8, near = 8.0 * vl, (2.0 * visc) * gv
        vb = combine(vl8 - near, -1.0 * (vl8 + near), -1.0 * vl, vl)
        vb = vb - visc * (((tv + rv) - 12.0 * lv) - 8.0 * gv)
        ub = ub + d_rows(L, "uu%d" % k)[0] - lu * L("xu%d" % k) - lv * L("xv%d" % k)
        vb = vb + d_rows(L, "uv%d" % k)[0] - lu * L("yu%d" % k) - lv * L("yv%d" % k)
        r = lu * u + lv * v
        rd = r * damp
        rE = r * E
        hbar = GRAV * (xlu + ylv) + rd * rH
        if with_h:
            xlh = d_rows(L, "lh%d" % k)[0]
            ylh = d_cols(L("lh%d" % k))[0]
            ub = ub + H * xlh
            vb = vb + H * ylh
            hbar = hbar + ADV * (u * xlh + v * ylh)
        ub = ADV * ub - (damp * lu + rE * u)
        vb = ADV * vb - (damp * lv + rE * v)
        return hbar, ub, vb, rd

    def keep_cot(L, St, k, lh, lu, lv):
        u = L("u%d" % k)
        St("lh%d" % k, lh)
        St("lu%d" % k, lu)
        St("lv%d" % k, lv)
        St("uu%d" % k, u * lu)
        St("uv%d" % k, u * lv)

    def add_drag(L, St, rd):
        St("acc", L("acc") - rd / (2.0 * L("c")))

    bb = [-(-(10 - 2 * k) // 8) for k in range(6)]
    for n in (1, 0):
        s, a, b = 3 * n, 3 * n + 1, 3 * n + 2
        top = n == 1

        def from_b(L, St):
            hbar, ub, vb, rd = pull(L, b, not top)
            add_drag(L, St, rd)
            quarter = 0.25 * L("w")
            new = [hbar if top else hbar + L("lh%d" % b), ub + L("lu%d" % b), vb + L("lv%d" % b)]
            keep_cot(L, St, a, *[quarter * x for x in new])

        sweep(bb[5 - b], from_b)

        def from_a(L, St):
            w = L("w")
            hbar, ub, vb, rd = pull(L, a, True)
            add_drag(L, St, rd)
            keep_cot(L, St, s, *[w * (x + L(y + str(a))) for x, y in zip((hbar, ub, vb), ("lh", "lu", "lv"))])

        sweep(bb[5 - a], from_a)

        def from_s(L, St):
            hbar, ub, vb, rd = pull(L, s, True)
            add_drag(L, St, rd)
            new = []
            for x, value in (("lh", hbar), ("lu", ub), ("lv", vb)):
                total = value + L(x + str(s)) + 3.0 * L(x + str(a))
                if not (top and x == "lh"):
                    total = total + 0.5 * L(x + str(b))
                new.append(total)
            if top:
                scale = (2.0 / 3.0) * L("w")
                keep_cot(L, St, 2, *[scale * x for x in new])
            else:
                for name, value in zip(("oh", "ou", "ov"), new):
                    St(name, value)

        sweep(bb[5 - s], from_s)

    shape = (2 * LANES, LANES)
    gather = column_at(shape, 0) == lax.broadcasted_iota(jnp.int32, shape, 1) + HALO
    gather = jnp.where(gather, 1.0, 0.0).astype(jnp.bfloat16)

    lane = lax.broadcasted_iota(jnp.int32, (rows, LANES), 1)
    in_tile = jnp.logical_and(lane >= HALO // 2, lane < (HALO + LANES) // 2)

    def own_columns(name):
        planes = [jnp.where(in_tile, S[at[name], t, OWN : OWN + rows, :], 0.0) for t in range(2)]
        return pick(jnp.concatenate(planes, axis=1), gather)

    for i, name in enumerate(("oh", "ou", "ov")):
        adj_ref[i] = own_columns(name)
    grad = own_columns("acc")
    grad_ref[...] = grad
    matched = farm_ref[...] == place_x * ny + place_y
    scale = 1.0 / (rows * LANES)
    own_sum_ref[0] = jnp.sum(jnp.where(matched, grad, 0.0)) * scale
    other_sum_ref[0] = jnp.sum(jnp.where(matched, 0.0, grad)) * scale


def shards(elevation, velocity, depth, turbine, wet_tiles, farm):
    rows = elevation.shape[0]
    counts = (lax.axis_size("gx"), lax.axis_size("gy"))
    nx, ny = counts
    wet = wet_tiles.reshape(1, 1)
    elev = elevation.reshape(rows, LANES)
    vel = velocity.reshape(2, rows, LANES)
    dep = depth.reshape(rows, LANES)
    turb = turbine.reshape(rows, LANES)
    farm_local = farm.reshape(rows, LANES)
    pairs_x = pairings(nx)
    pairs_y = pairings(ny)
    f32 = jnp.float32
    square = jax.ShapeDtypeStruct((LANES, LANES), f32)
    side = jax.ShapeDtypeStruct((rows, LANES), f32)
    corner = jax.ShapeDtypeStruct((HALO, LANES), f32)
    vmem = pl.BlockSpec(memory_space=pltpu.VMEM)
    smem = pl.BlockSpec(memory_space=pltpu.SMEM)
    shapes = [square] * len(pairs_x) + [side] * len(pairs_y) + [corner] * (len(pairs_x) * len(pairs_y))
    sent = pl.pallas_call(
        lambda *refs: pack_kernel(counts, *refs),
        out_shape=shapes,
        in_specs=[vmem] * 5,
        out_specs=[vmem] * len(shapes),
        name="pack",
    )(wet, elev, vel, dep, turb)
    sent = list(sent)
    row_got = [lax.ppermute(sent.pop(0), "gx", list(enumerate(p))) for p in pairs_x]
    side_got = [lax.ppermute(sent.pop(0), "gy", list(enumerate(p))) for p in pairs_y]
    corner_got = [
        [
            lax.ppermute(
                sent.pop(0),
                ("gx", "gy"),
                [(i * ny + j, px[i] * ny + py[j]) for i in range(nx) for j in range(ny)],
            )
            for py in pairs_y
        ]
        for px in pairs_x
    ]

    def left_right(got):
        if len(got) == 1:
            return got
        odd = lax.rem(lax.axis_index("gy"), 2) == 1
        return [jnp.where(odd, got[0], got[1]), jnp.where(odd, got[1], got[0])]

    edges = left_right(side_got)
    corners = [c for got in corner_got for c in left_right(got)]
    n_in = 6 + len(row_got) + len(edges) + len(corners)
    planes = 4 + 6 * 17 + 4
    adjoint, grad, own_sum, other_sum = pl.pallas_call(
        lambda *refs: main_kernel(counts, *refs),
        out_shape=[
            jax.ShapeDtypeStruct((3, rows, LANES), f32),
            side,
            jax.ShapeDtypeStruct((1,), f32),
            jax.ShapeDtypeStruct((1,), f32),
        ],
        in_specs=[vmem] * n_in,
        out_specs=[vmem, vmem, smem, smem],
        scratch_shapes=[pltpu.VMEM((planes, 2, rows + 2 * OWN, LANES), f32)],
        compiler_params=pltpu.CompilerParams(vmem_limit_bytes=40 * 1024 * 1024),
        name="adjoint",
    )(wet, elev, vel, dep, turb, farm_local, *row_got, *edges, *corners)
    passed = lax.ppermute(other_sum, "gx", [(i, (i + 1) % nx) for i in range(nx)])
    return (
        adjoint.reshape((3,) + elevation.shape),
        grad.reshape(elevation.shape),
        own_sum + passed,
    )


def solution(mesh):
    in_specs = (
        P("gx", None, "gy", None),
        P(None, "gx", None, "gy", None),
        P("gx", None, "gy", None),
        P("gx", None, "gy", None),
        P("gx", None, "gy"),
        P("gx", None, "gy", None),
    )
    out_specs = (P(None, "gx", None, "gy", None), P("gx", None, "gy", None), P(("gx", "gy")))
    return jax.shard_map(shards, mesh=mesh, in_specs=in_specs, out_specs=out_specs, check_vma=False)
```

time: 46.7 us -> 34.3 us (0.73)
  Pallas kernels: 25.7 us -> 13.4 us
    pallas_call x1, Pallas kernels: 23.8 us -> 11.5 us  [shards(): pl.pallas_call(lambda *refs: main_kernel(counts, *refs), out_shape=[jax.S...]
where the time goes in v1:
time: 34.3 us; the launch traced here: 34 us
  Pallas kernels  13.4 us (39%)
  starting transfers between devices  8.26 us (24%)
  waiting for transfers between devices  7.76 us (23%)
  between operations  3.76 us (11%)
  local copies, waits for them, and re-layouts  0.85 us (2%)
    pallas_call x1, Pallas kernels, shards(): pl.pallas_call(lambda *refs: main_kernel(counts, *refs), out_shape=[jax.S...  11.5 us
    ppermute x1, waiting for transfers between devices, shards(): lax.ppermute(other_sum, 'gx', [(i, (i + 1) % nx) for i in range(nx)])  5.36 us
    ppermute x2, starting transfers between devices, shards(): lax.ppermute(sent.pop(0), ('gx', 'gy'), [(i * ny + j, px[i] * ny + py[j])...  3.44 us
    ppermute x1, starting transfers between devices, shards(): lax.ppermute(sent.pop(0), 'gy', list(enumerate(p)))  2.52 us
    ppermute x2, waiting for transfers between devices, shards(): lax.ppermute(sent.pop(0), ('gx', 'gy'), [(i * ny + j, px[i] * ny + py[j])...  2.39 us
    ppermute x2, starting transfers between devices, shards(): lax.ppermute(sent.pop(0), 'gx', list(enumerate(p)))  1.94 us
    pallas_call x1, Pallas kernels, shards(): pl.pallas_call(lambda *refs: pack_kernel(counts, *refs), out_shape=shapes...  1.89 us
    unnamed x10, local copies, waits for them, and re-layouts  0.85 us
  transfers between devices with their start and end apart: 6, of which 3 were waited for; matrix products, arithmetic and copies ran while one was open for 0% of the time, Pallas kernels for 0%

profile of v1, /device:TPU:0, one launch (start us, length us, event | category | flops | bytes accessed | tf_op | source)
XLA Modules:
  0.0 34.0 jit_solution(13656079650184439015)
XLA Ops:
  1.3 0.0 copy-start
  1.3 0.0 copy-start.1
  1.3 0.0 copy-start.2
  1.3 0.0 copy-start.3
  1.3 1.9 %pack.1 = (f32[128,128]{1,0:T(8,128)}, f32[128,128]{1,0:T(8,128)}, f32[128,128]{1,0:T(8,128)}, f32[24,128]{1,0:T(8,128)}, f32[24,128]{1,0:T(8,128)}) custom-call(s32[1,1]{1,0:T(1,128)} %bitcast.12.refs_0_, f32[128,128]{1,0:T(8,128)} %bitcast.16, f32[2,128,128]{2,1,0:T(8,128)} %bitcast.14, f32[128,128]{1,0:T(8,128)} %bitcast.18, f32[128,128]{1,0:T(8,128)} %bitcast.20), custom_call_target="tpu_custom_call" | custom-call | tf_op jit(solution)/shard_map/pack/pallas_call | solution.py:464
  3.2 0.5 %collective-permute-start = (f32[128,128]{1,0:T(8,128)}, f32[128,128]{1,0:T(8,128)S(1)}, u32[]{:S(2)}, u32[]{:S(2)}) collective-permute-start(f32[128,128]{1,0:T(8,128)} %get-tuple-element.12), channel_id=1, source_target_pairs={{0,2},{2,0},{4,6},{6,4},{8,10},{10,8},{12,14},{14,12},{16,18},{18,... | collective-permute-start | bytes 196616 | tf_op jit(solution)/shard_map/ppermute | solution.py:472
  3.7 1.5 %collective-permute-start.1 = (f32[128,128]{1,0:T(8,128)}, f32[128,128]{1,0:T(8,128)S(1)}, u32[]{:S(2)}, u32[]{:S(2)}) collective-permute-start(f32[128,128]{1,0:T(8,128)} %get-tuple-element.13), channel_id=1, source_target_pairs={{0,0},{2,4},{4,2},{6,8},{8,6},{10,12},{12,10},{14,16},{16,14},{18,... | collective-permute-start | bytes 196616 | tf_op jit(solution)/shard_map/ppermute | solution.py:472
  5.1 2.5 %collective-permute-start.2 = (f32[128,128]{1,0:T(8,128)}, f32[128,128]{1,0:T(8,128)S(1)}, u32[]{:S(2)}, u32[]{:S(2)}) collective-permute-start(f32[128,128]{1,0:T(8,128)} %get-tuple-element.14), channel_id=1, source_target_pairs={{0,1},{1,0},{2,3},{3,2},{4,5},{5,4},{6,7},{7,6},{8,9},{9,8},{10,11... | collective-permute-start | bytes 196616 | tf_op jit(solution)/shard_map/ppermute | solution.py:473
  7.7 1.9 %collective-permute-start.3 = (f32[24,128]{1,0:T(8,128)}, f32[24,128]{1,0:T(8,128)S(1)}, u32[]{:S(2)}, u32[]{:S(2)}) collective-permute-start(f32[24,128]{1,0:T(8,128)} %get-tuple-element.15), channel_id=1, source_target_pairs={{0,3},{1,2},{2,1},{3,0},{4,7},{5,6},{6,5},{7,4},{8,11},{9,10},{10,... | collective-permute-start | bytes 36872 | tf_op jit(solution)/shard_map/ppermute | solution.py:476
  9.6 1.5 %collective-permute-start.4 = (f32[24,128]{1,0:T(8,128)}, f32[24,128]{1,0:T(8,128)S(1)}, u32[]{:S(2)}, u32[]{:S(2)}) collective-permute-start(f32[24,128]{1,0:T(8,128)} %get-tuple-element.16), channel_id=1, source_target_pairs={{0,1},{1,0},{2,5},{3,4},{4,3},{5,2},{6,9},{7,8},{8,7},{9,6},{10,13... | collective-permute-start | bytes 36872 | tf_op jit(solution)/shard_map/ppermute | solution.py:476
  11.1 0.8 %collective-permute-done.3.refs_9_ = f32[24,128]{1,0:T(8,128)S(1)} collective-permute-done((f32[24,128]{1,0:T(8,128)}, f32[24,128]{1,0:T(8,128)S(1)}, u32[]{:S(2)}, u32[]{:S(2)}) %collective-permute-start.3) | collective-permute-done | bytes 12320 | tf_op jit(solution)/shard_map/ppermute | solution.py:476
  11.9 1.6 %collective-permute-done.4.refs_10_ = f32[24,128]{1,0:T(8,128)S(1)} collective-permute-done((f32[24,128]{1,0:T(8,128)}, f32[24,128]{1,0:T(8,128)S(1)}, u32[]{:S(2)}, u32[]{:S(2)}) %collective-permute-start.4) | collective-permute-done | bytes 12320 | tf_op jit(solution)/shard_map/ppermute | solution.py:476
  13.5 0.0 collective-permute-done.refs_6_
  13.5 0.0 collective-permute-done.1.refs_7_
  13.5 0.0 collective-permute-done.2.refs_8_
  13.5 0.0 copy-done
  13.5 0.0 copy-done.1
  13.5 0.0 copy-done.2
  13.5 0.0 copy-done.3
  13.5 0.0 copy-start.4
  13.6 0.8 %copy-done.4 = s32[128,1,1,128]{3,2,1,0:T(1,128)S(1)} copy-done((s32[128,1,1,128]{3,2,1,0:T(1,128)S(1)}, s32[128,1,1,128]{3,2,1,0:T(1,128)}, u32[]{:S(2)}) %copy-start.4) | copy-done | bytes 65560
  14.4 11.5 %adjoint.1 = (f32[3,128,128]{2,1,0:T(8,128)}, f32[128,128]{1,0:T(8,128)}, f32[1]{0:T(128)}, f32[1]{0:T(128)}) custom-call(s32[1,1]{1,0:T(1,128)} %bitcast.13.refs_0_, f32[128,128]{1,0:T(8,128)S(1)} %bitcast.17, f32[2,128,128]{2,1,0:T(8,128)S(1)} %bitcast.15, f32[128,128]{1,0:T(8,128)S(1)} %bitcast.19, f32[128,128]{1,0:T(8,128)S(1)} %bitcast.21, ...), custom_call_target="tpu_custom_call" | custom-call | tf_op jit(solution)/shard_map/adjoint/pallas_call | solution.py:496
  25.9 0.4 %collective-permute-start.5 = (f32[1]{0:T(128)}, f32[1]{0:T(128)}, u32[]{:S(2)}, u32[]{:S(2)}) collective-permute-start(f32[1]{0:T(128)} %get-tuple-element.20), channel_id=1, source_target_pairs={{0,2},{2,4},{4,6},{6,8},{8,10},{10,12},{12,14},{14,16},{16,18},{18... | collective-permute-start | bytes 20 | tf_op jit(solution)/shard_map/ppermute | solution.py:510
  26.3 5.4 %collective-permute-done.5 = f32[1]{0:T(128)} collective-permute-done((f32[1]{0:T(128)}, f32[1]{0:T(128)}, u32[]{:S(2)}, u32[]{:S(2)}) %collective-permute-start.5) | collective-permute-done | bytes 36 | tf_op jit(solution)/shard_map/ppermute | solution.py:510
Async XLA Ops:
  1.3 12.2 %copy-start = (f32[2,128,1,1,128]{4,3,2,1,0:T(1,128)S(1)}, f32[2,128,1,1,128]{4,3,2,1,0:T(1,128)}, u32[]{:S(2)}) copy-start(f32[2,128,1,1,128]{4,3,2,1,0:T(1,128)} %param.7) | copy-start | bytes 393220
  1.3 12.2 %copy-start.1 = (f32[128,1,1,128]{3,2,1,0:T(1,128)S(1)}, f32[128,1,1,128]{3,2,1,0:T(1,128)}, u32[]{:S(2)}) copy-start(f32[128,1,1,128]{3,2,1,0:T(1,128)} %param.6) | copy-start | bytes 196612
  1.3 12.2 %copy-start.2 = (f32[128,1,1,128]{3,2,1,0:T(1,128)S(1)}, f32[128,1,1,128]{3,2,1,0:T(1,128)}, u32[]{:S(2)}) copy-start(f32[128,1,1,128]{3,2,1,0:T(1,128)} %param.8) | copy-start | bytes 196612
  1.3 12.2 %copy-start.3 = (f32[128,1,1,128]{3,2,1,0:T(1,128)S(1)}, f32[128,1,1,128]{3,2,1,0:T(1,128)}, u32[]{:S(2)}) copy-start(f32[128,1,1,128]{3,2,1,0:T(1,128)} %param.9) | copy-start | bytes 196612
  3.2 10.3 %collective-permute-start = (f32[128,128]{1,0:T(8,128)}, f32[128,128]{1,0:T(8,128)S(1)}, u32[]{:S(2)}, u32[]{:S(2)}) collective-permute-start(f32[128,128]{1,0:T(8,128)} %get-tuple-element.12), channel_id=1, source_target_pairs={{0,2},{2,0},{4,6},{6,4},{8,10},{10,8},{12,14},{14,12},{16,18},{18,... | collective-permute-start | bytes 196616 | tf_op jit(solution)/shard_map/ppermute | solution.py:472
  3.7 9.8 %collective-permute-start.1 = (f32[128,128]{1,0:T(8,128)}, f32[128,128]{1,0:T(8,128)S(1)}, u32[]{:S(2)}, u32[]{:S(2)}) collective-permute-start(f32[128,128]{1,0:T(8,128)} %get-tuple-element.13), channel_id=1, source_target_pairs={{0,0},{2,4},{4,2},{6,8},{8,6},{10,12},{12,10},{14,16},{16,14},{18,... | collective-permute-start | bytes 196616 | tf_op jit(solution)/shard_map/ppermute | solution.py:472
  5.1 8.4 %collective-permute-start.2 = (f32[128,128]{1,0:T(8,128)}, f32[128,128]{1,0:T(8,128)S(1)}, u32[]{:S(2)}, u32[]{:S(2)}) collective-permute-start(f32[128,128]{1,0:T(8,128)} %get-tuple-element.14), channel_id=1, source_target_pairs={{0,1},{1,0},{2,3},{3,2},{4,5},{5,4},{6,7},{7,6},{8,9},{9,8},{10,11... | collective-permute-start | bytes 196616 | tf_op jit(solution)/shard_map/ppermute | solution.py:473
  7.7 4.2 %collective-permute-start.3 = (f32[24,128]{1,0:T(8,128)}, f32[24,128]{1,0:T(8,128)S(1)}, u32[]{:S(2)}, u32[]{:S(2)}) collective-permute-start(f32[24,128]{1,0:T(8,128)} %get-tuple-element.15), channel_id=1, source_target_pairs={{0,3},{1,2},{2,1},{3,0},{4,7},{5,6},{6,5},{7,4},{8,11},{9,10},{10,... | collective-permute-start | bytes 36872 | tf_op jit(solution)/shard_map/ppermute | solution.py:476
  9.6 3.9 %collective-permute-start.4 = (f32[24,128]{1,0:T(8,128)}, f32[24,128]{1,0:T(8,128)S(1)}, u32[]{:S(2)}, u32[]{:S(2)}) collective-permute-start(f32[24,128]{1,0:T(8,128)} %get-tuple-element.16), channel_id=1, source_target_pairs={{0,1},{1,0},{2,5},{3,4},{4,3},{5,2},{6,9},{7,8},{8,7},{9,6},{10,13... | collective-permute-start | bytes 36872 | tf_op jit(solution)/shard_map/ppermute | solution.py:476
  13.5 0.8 %copy-start.4 = (s32[128,1,1,128]{3,2,1,0:T(1,128)S(1)}, s32[128,1,1,128]{3,2,1,0:T(1,128)}, u32[]{:S(2)}) copy-start(s32[128,1,1,128]{3,2,1,0:T(1,128)} %param.11) | copy-start | bytes 196612
  25.9 5.7 %collective-permute-start.5 = (f32[1]{0:T(128)}, f32[1]{0:T(128)}, u32[]{:S(2)}, u32[]{:S(2)}) collective-permute-start(f32[1]{0:T(128)} %get-tuple-element.20), channel_id=1, source_target_pairs={{0,2},{2,4},{4,6},{6,8},{8,10},{10,12},{12,14},{14,16},{16,18},{18... | collective-permute-start | bytes 20 | tf_op jit(solution)/shard_map/ppermute | solution.py:510

commit v2 on v1

--- a/solution.py
+++ b/solution.py
@@ -13,7 +13,6 @@
 OWN = GUARD + HALO
 FIELDS = 5
 STEP = 16
-UNROLL = 2
 WIDE = LANES + 2 * HALO
 ADV = 0.1 / 12.0
 GRAV = 0.3 / 12.0
@@ -40,14 +39,15 @@
     return result
 
 
-def pack_kernel(counts, wet_ref, elev_ref, vel_ref, depth_ref, turb_ref, *outs):
+def pack_kernel(counts, wet_ref, elev_ref, vel_ref, depth_ref, turb_ref, farm_ref, *outs):
     rows = elev_ref.shape[0]
     fields = [elev_ref[...], vel_ref[0], vel_ref[1], depth_ref[...], turb_ref[...]]
     refs = [elev_ref, vel_ref.at[0], vel_ref.at[1], depth_ref, turb_ref]
-    wet = wet_ref[...].astype(jnp.float32)
+    wet = wet_ref[0].astype(jnp.float32)
     roles_x = roles("gx", counts[0])
     roles_y = roles("gy", counts[1])
     outs = list(outs)
+    outs.pop()[...] = jnp.broadcast_to(wet, (8, LANES))
     row_outs = [outs.pop(0) for _ in roles_x]
     side_outs = [outs.pop(0) for _ in roles_y]
     starts = [pl.multiple_of(after * (rows - HALO), 8) for after, _ in roles_x]
@@ -146,12 +146,14 @@
     sides = 1 if ny == 2 else 2
     side_in = [rest.pop(0) for _ in range(sides)]
     corner_in = [[rest.pop(0) for _ in range(sides)] for _ in roles_x]
-    adj_ref, grad_ref, own_sum_ref, other_sum_ref, S = rest
+    adj_ref, grad_ref, own_sum_ref, other_sum_ref, S, farm_here, farm_sem = rest
+    farm_copy = pltpu.make_async_copy(farm_ref, farm_here, farm_sem)
+    farm_copy.start()
     place_x = lax.axis_index("gx")
     place_y = lax.axis_index("gy")
     has_left = place_y > 0
     has_right = place_y < ny - 1
-    wet = wet_ref[...].astype(jnp.float32)
+    wet = wet_ref[:1, :1]
 
     names = ["w", "T", "c", "d"]
     for k in range(6):
@@ -242,13 +244,7 @@
 
             body(load, store)
 
-        def step(i, carry):
-            for k in range(UNROLL):
-                chunk(pl.multiple_of(OWN - 8 * blocks + (i * UNROLL + k) * STEP, 8))
-            return carry
-
-        lax.fori_loop(0, count // UNROLL, step, 0)
-        for k in range(count // UNROLL * UNROLL, count):
+        for k in range(count):
             chunk(OWN - 8 * blocks + k * STEP)
 
     def d_rows(L, name):
@@ -436,17 +432,18 @@
         adj_ref[i] = own_columns(name)
     grad = own_columns("acc")
     grad_ref[...] = grad
-    matched = farm_ref[...] == place_x * ny + place_y
+    farm_copy.wait()
+    matched = farm_here[...] == place_x * ny + place_y
     scale = 1.0 / (rows * LANES)
-    own_sum_ref[0] = jnp.sum(jnp.where(matched, grad, 0.0)) * scale
-    other_sum_ref[0] = jnp.sum(jnp.where(matched, 0.0, grad)) * scale
+    for ref, part in ((own_sum_ref, jnp.where(matched, grad, 0.0)), (other_sum_ref, jnp.where(matched, 0.0, grad))):
+        total = jnp.sum(jnp.sum(part, axis=0, keepdims=True), axis=1, keepdims=True) * scale
+        ref[...] = jnp.broadcast_to(total, (1, LANES))
 
 
 def shards(elevation, velocity, depth, turbine, wet_tiles, farm):
     rows = elevation.shape[0]
     counts = (lax.axis_size("gx"), lax.axis_size("gy"))
     nx, ny = counts
-    wet = wet_tiles.reshape(1, 1)
     elev = elevation.reshape(rows, LANES)
     vel = velocity.reshape(2, rows, LANES)
     dep = depth.reshape(rows, LANES)
@@ -459,16 +456,17 @@
     side = jax.ShapeDtypeStruct((rows, LANES), f32)
     corner = jax.ShapeDtypeStruct((HALO, LANES), f32)
     vmem = pl.BlockSpec(memory_space=pltpu.VMEM)
-    smem = pl.BlockSpec(memory_space=pltpu.SMEM)
     shapes = [square] * len(pairs_x) + [side] * len(pairs_y) + [corner] * (len(pairs_x) * len(pairs_y))
+    shapes.append(jax.ShapeDtypeStruct((8, LANES), f32))
     sent = pl.pallas_call(
         lambda *refs: pack_kernel(counts, *refs),
         out_shape=shapes,
-        in_specs=[vmem] * 5,
+        in_specs=[vmem] * 5 + [pl.BlockSpec(memory_space=pl.ANY)],
         out_specs=[vmem] * len(shapes),
         name="pack",
-    )(wet, elev, vel, dep, turb)
+    )(wet_tiles, elev, vel, dep, turb, farm_local)
     sent = list(sent)
+    wet = sent.pop()
     row_got = [lax.ppermute(sent.pop(0), "gx", list(enumerate(p))) for p in pairs_x]
     side_got = [lax.ppermute(sent.pop(0), "gy", list(enumerate(p))) for p in pairs_y]
     corner_got = [
@@ -498,12 +496,16 @@
         out_shape=[
             jax.ShapeDtypeStruct((3, rows, LANES), f32),
             side,
-            jax.ShapeDtypeStruct((1,), f32),
-            jax.ShapeDtypeStruct((1,), f32),
+            jax.ShapeDtypeStruct((1, LANES), f32),
+            jax.ShapeDtypeStruct((1, LANES), f32),
         ],
-        in_specs=[vmem] * n_in,
-        out_specs=[vmem, vmem, smem, smem],
-        scratch_shapes=[pltpu.VMEM((planes, 2, rows + 2 * OWN, LANES), f32)],
+        in_specs=[vmem] * 5 + [pl.BlockSpec(memory_space=pl.ANY)] + [vmem] * (n_in - 6),
+        out_specs=[vmem] * 4,
+        scratch_shapes=[
+            pltpu.VMEM((planes, 2, rows + 2 * OWN, LANES), f32),
+            pltpu.VMEM((rows, LANES), jnp.int32),
+            pltpu.SemaphoreType.DMA,
+        ],
         compiler_params=pltpu.CompilerParams(vmem_limit_bytes=40 * 1024 * 1024),
         name="adjoint",
     )(wet, elev, vel, dep, turb, farm_local, *row_got, *edges, *corners)
@@ -511,7 +513,7 @@
     return (
         adjoint.reshape((3,) + elevation.shape),
         grad.reshape(elevation.shape),
-        own_sum + passed,
+        (own_sum + passed)[0, :1],
     )
 
 

time: 34.3 us -> 29.9 us (0.87)
  between operations: 3.76 us -> 1.38 us
  Pallas kernels: 13.4 us -> 11.7 us
  local copies, waits for them, and re-layouts: 0.85 us -> 0.02 us
  other arithmetic: 0 us -> 0.51 us
    pallas_call x1, Pallas kernels: 11.5 us -> 9.82 us  [shards(): pl.pallas_call(lambda *refs: main_kernel(counts, *refs), out_shape=[jax.S...]
    unnamed x10 -> x12, local copies, waits for them, and re-layouts: 0.85 us -> 0.02 us
    add x0 -> x1, other arithmetic: none -> 0.51 us  [shards(): own_sum + passed]
where the time goes in v2:
time: 29.9 us; the launch traced here: 29.7 us
  Pallas kernels  11.7 us (39%)
  starting transfers between devices  8.27 us (28%)
  waiting for transfers between devices  7.75 us (26%)
  between operations  1.38 us (5%)
  other arithmetic  0.51 us (2%)
    pallas_call x1, Pallas kernels, shards(): pl.pallas_call(lambda *refs: main_kernel(counts, *refs), out_shape=[jax.S...  9.82 us
    ppermute x1, waiting for transfers between devices, shards(): lax.ppermute(other_sum, 'gx', [(i, (i + 1) % nx) for i in range(nx)])  5.36 us
    ppermute x2, starting transfers between devices, shards(): lax.ppermute(sent.pop(0), ('gx', 'gy'), [(i * ny + j, px[i] * ny + py[j])...  3.44 us
    ppermute x1, starting transfers between devices, shards(): lax.ppermute(sent.pop(0), 'gy', list(enumerate(p)))  2.41 us
    ppermute x2, waiting for transfers between devices, shards(): lax.ppermute(sent.pop(0), ('gx', 'gy'), [(i * ny + j, px[i] * ny + py[j])...  2.39 us
    ppermute x2, starting transfers between devices, shards(): lax.ppermute(sent.pop(0), 'gx', list(enumerate(p)))  2.07 us
    pallas_call x1, Pallas kernels, shards(): pl.pallas_call(lambda *refs: pack_kernel(counts, *refs), out_shape=shapes...  1.9 us
  transfers between devices with their start and end apart: 6, of which 3 were waited for; matrix products, arithmetic and copies ran while one was open for 0% of the time, Pallas kernels for 0%

profile of v2, /device:TPU:0, one launch (start us, length us, event | category | flops | bytes accessed | tf_op | source)
XLA Modules:
  0.0 29.7 jit_solution(329482097334695437)
XLA Ops:
  1.3 0.0 copy-start
  1.3 0.0 copy-start.1
  1.3 0.0 copy-start.2
  1.3 0.0 copy-start.3
  1.3 0.0 copy-start.4
  1.3 1.9 %pack.1 = (f32[128,128]{1,0:T(8,128)}, f32[128,128]{1,0:T(8,128)}, f32[128,128]{1,0:T(8,128)}, f32[24,128]{1,0:T(8,128)}, f32[24,128]{1,0:T(8,128)}, /*index=5*/f32[8,128]{1,0:T(8,128)}) custom-call(s32[1,1,1]{2,1,0:T(1,128)S(6)} %copy.11.refs_0_, f32[128,128]{1,0:T(8,128)} %bitcast.15, f32[2,128,128]{2,1,0:T(8,128)} %bitcast.13, f32[128,128]{1,0:T(8,128)} %bitcast.17, ...), custom_call_target="tpu_custom_call" | custom-call | tf_op jit(solution)/shard_map/pack/pallas_call | solution.py:461
  3.2 0.5 %collective-permute-start = (f32[128,128]{1,0:T(8,128)}, f32[128,128]{1,0:T(8,128)S(1)}, u32[]{:S(2)}, u32[]{:S(2)}) collective-permute-start(f32[128,128]{1,0:T(8,128)} %get-tuple-element.14), channel_id=1, source_target_pairs={{0,2},{2,0},{4,6},{6,4},{8,10},{10,8},{12,14},{14,12},{16,18},{18,... | collective-permute-start | bytes 196616 | tf_op jit(solution)/shard_map/ppermute | solution.py:470
  3.7 1.6 %collective-permute-start.1 = (f32[128,128]{1,0:T(8,128)}, f32[128,128]{1,0:T(8,128)S(1)}, u32[]{:S(2)}, u32[]{:S(2)}) collective-permute-start(f32[128,128]{1,0:T(8,128)} %get-tuple-element.15), channel_id=1, source_target_pairs={{0,0},{2,4},{4,2},{6,8},{8,6},{10,12},{12,10},{14,16},{16,14},{18,... | collective-permute-start | bytes 196616 | tf_op jit(solution)/shard_map/ppermute | solution.py:470
  5.3 2.4 %collective-permute-start.2 = (f32[128,128]{1,0:T(8,128)}, f32[128,128]{1,0:T(8,128)S(1)}, u32[]{:S(2)}, u32[]{:S(2)}) collective-permute-start(f32[128,128]{1,0:T(8,128)} %get-tuple-element.16), channel_id=1, source_target_pairs={{0,1},{1,0},{2,3},{3,2},{4,5},{5,4},{6,7},{7,6},{8,9},{9,8},{10,11... | collective-permute-start | bytes 196616 | tf_op jit(solution)/shard_map/ppermute | solution.py:471
  7.7 1.9 %collective-permute-start.3 = (f32[24,128]{1,0:T(8,128)}, f32[24,128]{1,0:T(8,128)S(1)}, u32[]{:S(2)}, u32[]{:S(2)}) collective-permute-start(f32[24,128]{1,0:T(8,128)} %get-tuple-element.17), channel_id=1, source_target_pairs={{0,3},{1,2},{2,1},{3,0},{4,7},{5,6},{6,5},{7,4},{8,11},{9,10},{10,... | collective-permute-start | bytes 36872 | tf_op jit(solution)/shard_map/ppermute | solution.py:474
  9.6 1.5 %collective-permute-start.4 = (f32[24,128]{1,0:T(8,128)}, f32[24,128]{1,0:T(8,128)S(1)}, u32[]{:S(2)}, u32[]{:S(2)}) collective-permute-start(f32[24,128]{1,0:T(8,128)} %get-tuple-element.18), channel_id=1, source_target_pairs={{0,1},{1,0},{2,5},{3,4},{4,3},{5,2},{6,9},{7,8},{8,7},{9,6},{10,13... | collective-permute-start | bytes 36872 | tf_op jit(solution)/shard_map/ppermute | solution.py:474
  11.1 0.8 %collective-permute-done.3.refs_9_ = f32[24,128]{1,0:T(8,128)S(1)} collective-permute-done((f32[24,128]{1,0:T(8,128)}, f32[24,128]{1,0:T(8,128)S(1)}, u32[]{:S(2)}, u32[]{:S(2)}) %collective-permute-start.3) | collective-permute-done | bytes 12320 | tf_op jit(solution)/shard_map/ppermute | solution.py:474
  11.9 1.6 %collective-permute-done.4.refs_10_ = f32[24,128]{1,0:T(8,128)S(1)} collective-permute-done((f32[24,128]{1,0:T(8,128)}, f32[24,128]{1,0:T(8,128)S(1)}, u32[]{:S(2)}, u32[]{:S(2)}) %collective-permute-start.4) | collective-permute-done | bytes 12320 | tf_op jit(solution)/shard_map/ppermute | solution.py:474
  13.5 0.0 collective-permute-done.refs_6_
  13.5 0.0 collective-permute-done.1.refs_7_
  13.5 0.0 collective-permute-done.2.refs_8_
  13.5 0.0 copy-done
  13.6 0.0 copy-done.1
  13.6 0.0 copy-done.2
  13.6 0.0 copy-done.3
  13.6 9.8 %adjoint.1 = (f32[3,128,128]{2,1,0:T(8,128)}, f32[128,128]{1,0:T(8,128)}, f32[1,128]{1,0:T(1,128)S(1)}, f32[1,128]{1,0:T(1,128)S(1)}) custom-call(f32[8,128]{1,0:T(8,128)S(1)} %copy-done.5, f32[128,128]{1,0:T(8,128)S(1)} %bitcast.16, f32[2,128,128]{2,1,0:T(8,128)S(1)} %bitcast.14, f32[128,128]{1,0:T(8,128)S(1)} %bitcast.18, f32[128,128]{1,0:T(8,128)S(1)} %bitcast.20, ...), custom_call_target="tpu_custom_call" | custom-call | tf_op jit(solution)/shard_map/adjoint/pallas_call | solution.py:494
  23.4 0.4 %collective-permute-start.5 = (f32[1,128]{1,0:T(1,128)S(1)}, f32[1,128]{1,0:T(1,128)S(1)}, u32[]{:S(2)}, u32[]{:S(2)}) collective-permute-start(f32[1,128]{1,0:T(1,128)S(1)} %get-tuple-element.22), channel_id=1, source_target_pairs={{0,2},{2,4},{4,6},{6,8},{8,10},{10,12},{12,14},{14,16},{16,18},{18... | collective-permute-start | bytes 1544 | tf_op jit(solution)/shard_map/ppermute | solution.py:512
  23.8 5.4 %collective-permute-done.5 = f32[1,128]{1,0:T(1,128)S(1)} collective-permute-done((f32[1,128]{1,0:T(1,128)S(1)}, f32[1,128]{1,0:T(1,128)S(1)}, u32[]{:S(2)}, u32[]{:S(2)}) %collective-permute-start.5) | collective-permute-done | bytes 544 | tf_op jit(solution)/shard_map/ppermute | solution.py:512
  29.2 0.5 %add.3 = f32[1,128]{1,0:T(1,128)} add(f32[1,128]{1,0:T(1,128)S(1)} %get-tuple-element.21, f32[1,128]{1,0:T(1,128)S(1)} %collective-permute-done.5) | non-fusion elementwise | flops 128 | bytes 1536 | tf_op jit(solution)/shard_map/add | solution.py:516
  (3 shorter events, 0.0 us)
Async XLA Ops:
  1.3 12.3 %copy-start = (f32[2,128,1,1,128]{4,3,2,1,0:T(1,128)S(1)}, f32[2,128,1,1,128]{4,3,2,1,0:T(1,128)}, u32[]{:S(2)}) copy-start(f32[2,128,1,1,128]{4,3,2,1,0:T(1,128)} %param.7) | copy-start | bytes 393220
  1.3 12.3 %copy-start.1 = (f32[128,1,1,128]{3,2,1,0:T(1,128)S(1)}, f32[128,1,1,128]{3,2,1,0:T(1,128)}, u32[]{:S(2)}) copy-start(f32[128,1,1,128]{3,2,1,0:T(1,128)} %param.6) | copy-start | bytes 196612
  1.3 12.3 %copy-start.2 = (f32[128,1,1,128]{3,2,1,0:T(1,128)S(1)}, f32[128,1,1,128]{3,2,1,0:T(1,128)}, u32[]{:S(2)}) copy-start(f32[128,1,1,128]{3,2,1,0:T(1,128)} %param.8) | copy-start | bytes 196612
  1.3 12.3 %copy-start.3 = (f32[128,1,1,128]{3,2,1,0:T(1,128)S(1)}, f32[128,1,1,128]{3,2,1,0:T(1,128)}, u32[]{:S(2)}) copy-start(f32[128,1,1,128]{3,2,1,0:T(1,128)} %param.9) | copy-start | bytes 196612
  1.3 12.3 %copy-start.4 = (s32[128,1,1,128]{3,2,1,0:T(1,128)S(1)}, s32[128,1,1,128]{3,2,1,0:T(1,128)}, u32[]{:S(2)}) copy-start(s32[128,1,1,128]{3,2,1,0:T(1,128)} %param.11) | copy-start | bytes 196612
  3.2 10.3 %collective-permute-start = (f32[128,128]{1,0:T(8,128)}, f32[128,128]{1,0:T(8,128)S(1)}, u32[]{:S(2)}, u32[]{:S(2)}) collective-permute-start(f32[128,128]{1,0:T(8,128)} %get-tuple-element.14), channel_id=1, source_target_pairs={{0,2},{2,0},{4,6},{6,4},{8,10},{10,8},{12,14},{14,12},{16,18},{18,... | collective-permute-start | bytes 196616 | tf_op jit(solution)/shard_map/ppermute | solution.py:470
  3.7 9.9 %copy-start.5 = (f32[8,128]{1,0:T(8,128)S(1)}, f32[8,128]{1,0:T(8,128)}, u32[]{:S(2)}) copy-start(f32[8,128]{1,0:T(8,128)} %get-tuple-element.13.refs_0_) | copy-start | bytes 12292
  3.7 9.9 %collective-permute-start.1 = (f32[128,128]{1,0:T(8,128)}, f32[128,128]{1,0:T(8,128)S(1)}, u32[]{:S(2)}, u32[]{:S(2)}) collective-permute-start(f32[128,128]{1,0:T(8,128)} %get-tuple-element.15), channel_id=1, source_target_pairs={{0,0},{2,4},{4,2},{6,8},{8,6},{10,12},{12,10},{14,16},{16,14},{18,... | collective-permute-start | bytes 196616 | tf_op jit(solution)/shard_map/ppermute | solution.py:470
  5.3 8.2 %collective-permute-start.2 = (f32[128,128]{1,0:T(8,128)}, f32[128,128]{1,0:T(8,128)S(1)}, u32[]{:S(2)}, u32[]{:S(2)}) collective-permute-start(f32[128,128]{1,0:T(8,128)} %get-tuple-element.16), channel_id=1, source_target_pairs={{0,1},{1,0},{2,3},{3,2},{4,5},{5,4},{6,7},{7,6},{8,9},{9,8},{10,11... | collective-permute-start | bytes 196616 | tf_op jit(solution)/shard_map/ppermute | solution.py:471
  7.7 4.2 %collective-permute-start.3 = (f32[24,128]{1,0:T(8,128)}, f32[24,128]{1,0:T(8,128)S(1)}, u32[]{:S(2)}, u32[]{:S(2)}) collective-permute-start(f32[24,128]{1,0:T(8,128)} %get-tuple-element.17), channel_id=1, source_target_pairs={{0,3},{1,2},{2,1},{3,0},{4,7},{5,6},{6,5},{7,4},{8,11},{9,10},{10,... | collective-permute-start | bytes 36872 | tf_op jit(solution)/shard_map/ppermute | solution.py:474
  9.6 3.9 %collective-permute-start.4 = (f32[24,128]{1,0:T(8,128)}, f32[24,128]{1,0:T(8,128)S(1)}, u32[]{:S(2)}, u32[]{:S(2)}) collective-permute-start(f32[24,128]{1,0:T(8,128)} %get-tuple-element.18), channel_id=1, source_target_pairs={{0,1},{1,0},{2,5},{3,4},{4,3},{5,2},{6,9},{7,8},{8,7},{9,6},{10,13... | collective-permute-start | bytes 36872 | tf_op jit(solution)/shard_map/ppermute | solution.py:474
  23.4 5.7 %collective-permute-start.5 = (f32[1,128]{1,0:T(1,128)S(1)}, f32[1,128]{1,0:T(1,128)S(1)}, u32[]{:S(2)}, u32[]{:S(2)}) collective-permute-start(f32[1,128]{1,0:T(1,128)S(1)} %get-tuple-element.22), channel_id=1, source_target_pairs={{0,2},{2,4},{4,6},{6,8},{8,10},{10,12},{12,14},{14,16},{16,18},{18... | collective-permute-start | bytes 1544 | tf_op jit(solution)/shard_map/ppermute | solution.py:512

commit v3 on v2

v3 whole, which is shorter than its diff:
```python
import jax
import jax.numpy as jnp
from jax import lax
from jax.experimental import pallas as pl
from jax.experimental.pallas import tpu as pltpu
from jax.sharding import PartitionSpec as P

SPEED_EPS = 0.01
BED_DRAG = 0.1
LANES = 128
HALO = 24
GUARD = 8
OWN = GUARD + HALO
FIELDS = 5
STEP = 16
VMEM_MAIN = 36 * 1024 * 1024
VMEM_OWN = 36 * 1024 * 1024
VMEM_LAST = 12 * 1024 * 1024
WIDE = LANES + 2 * HALO
ADV = 0.1 / 12.0
GRAV_RATIO = 3.0
VISC = 0.004 / ADV
EDGE = 4


def pairings(count):
    even = [i ^ 1 for i in range(count)]
    if count == 2:
        return [even]
    odd = [i if i in (0, count - 1) else ((i + 1) ^ 1) - 1 for i in range(count)]
    return [even, odd]


def roles(axis, count):
    place = lax.axis_index(axis)
    odd = lax.rem(place, 2)
    after_a = 1 - odd
    result = [(after_a, True)]
    if count > 2:
        after_b = odd
        exists = jnp.where(after_b == 1, place < count - 1, place > 0)
        result.append((after_b, exists))
    return result


def pack_kernel(counts, wet_ref, elev_ref, vel_ref, depth_ref, turb_ref, farm_ref, *outs):
    rows = elev_ref.shape[0]
    fields = [elev_ref[...], vel_ref[0], vel_ref[1], depth_ref[...], turb_ref[...]]
    refs = [elev_ref, vel_ref.at[0], vel_ref.at[1], depth_ref, turb_ref]
    wet = wet_ref[0].astype(jnp.float32)
    roles_x = roles("gx", counts[0])
    roles_y = roles("gy", counts[1])
    outs = list(outs)
    stack = outs.pop()
    for f, field in enumerate(fields):
        stack[rows * f : rows * (f + 1), :] = field
    own = lax.axis_index("gx") * counts[1] + lax.axis_index("gy")
    stack[rows * FIELDS : rows * (FIELDS + 1), :] = jnp.where(farm_ref[...] == own, 1.0, 0.0)
    stack[rows * (FIELDS + 1) :, :] = jnp.broadcast_to(wet, (8, LANES))
    row_outs = [outs.pop(0) for _ in roles_x]
    side_outs = [outs.pop(0) for _ in roles_y]
    starts = [pl.multiple_of(after * (rows - HALO), 8) for after, _ in roles_x]
    for start, out in zip(starts, row_outs):
        for f, ref in enumerate(refs):
            out[HALO * f : HALO * (f + 1), :] = ref[pl.ds(start, HALO), :]
        out[HALO * FIELDS :, :] = jnp.broadcast_to(wet, (LANES - HALO * FIELDS, LANES))
    lane = lax.broadcasted_iota(jnp.int32, (rows, LANES), 1)
    for (after, _), out in zip(roles_y, side_outs):
        packed = jnp.broadcast_to(wet, (rows, LANES))
        for f in reversed(range(FIELDS)):
            moved = jnp.where(
                after == 1,
                pltpu.roll(fields[f], HALO * (f + 1), 1),
                pltpu.roll(fields[f], HALO * f, 1),
            )
            packed = jnp.where(lane < HALO * (f + 1), moved, packed)
        out[...] = packed
    for start in starts:
        for side in side_outs:
            outs.pop(0)[...] = side[pl.ds(start, HALO), :]


class Pair:
    def __init__(self, even, odd):
        self.even, self.odd = even, odd

    def map(self, function):
        return Pair(function(self.even), function(self.odd))

    def __add__(self, other):
        return both(self, other, lambda a, b: a + b)

    def __sub__(self, other):
        return both(self, other, lambda a, b: a - b)

    def __mul__(self, other):
        return both(self, other, lambda a, b: a * b)

    def __truediv__(self, other):
        return both(self, other, lambda a, b: a / b)

    def __rmul__(self, other):
        return self.map(lambda a: other * a)


def both(a, b, function):
    if isinstance(b, Pair):
        return Pair(function(a.even, b.even), function(a.odd, b.odd))
    return Pair(function(a.even, b), function(a.odd, b))


def after(x):
    return pltpu.roll(x, LANES - 1, 1)


def before(x):
    return pltpu.roll(x, 1, 1)


def d_cols(f):
    ea, eb, oa, ob = after(f.even), before(f.even), after(f.odd), before(f.odd)
    slope = Pair(
        8.0 * (f.odd - ob) - (ea - eb),
        8.0 * (ea - f.even) - (oa - ob),
    )
    return slope, Pair(ea + eb, oa + ob)


def combine(p1, m1, p2, m2):
    return Pair(
        (p1.odd - after(p2.even)) - before(m1.odd - m2.even),
        (after(p1.even - p2.odd) - m1.even) + before(m2.odd),
    )


def thirds(x):
    one = x.astype(jnp.bfloat16)
    rest = x - one.astype(jnp.float32)
    two = rest.astype(jnp.bfloat16)
    three = (rest - two.astype(jnp.float32)).astype(jnp.bfloat16)
    return one, two, three


def pick(parts, chosen):
    got = [jnp.dot(part, chosen, preferred_element_type=jnp.float32) for part in parts]
    return (got[0] + got[1]) + got[2]


def column_at(shape, dim):
    place = lax.broadcasted_iota(jnp.int32, shape, dim)
    return 2 * lax.rem(place, LANES) + lax.div(place, LANES)


def own_columns(rows, planes):
    shape = (2 * LANES, LANES)
    gather = column_at(shape, 0) == lax.broadcasted_iota(jnp.int32, shape, 1) + HALO
    gather = jnp.where(gather, 1.0, 0.0).astype(jnp.bfloat16)
    lane = lax.broadcasted_iota(jnp.int32, (rows, LANES), 1)
    in_tile = jnp.logical_and(lane >= HALO // 2, lane < (HALO + LANES) // 2)
    both_planes = jnp.concatenate([jnp.where(in_tile, x, 0.0) for x in planes], axis=1)
    return pick(thirds(both_planes), gather)


def place_of(names, ref):
    return {name: (ref, i) for i, name in enumerate(names)}


SAVED = ("u", "v", "H", "xu", "xv", "yu", "yv", "dm", "om", "E", "rH")
COTANGENT = ("lh", "lu", "lv", "uu", "uv")
KEPT = [x + "0" for x in SAVED + COTANGENT] + [x + k for k in "12" for x in ("lh", "lu", "lv")]
PLANES = (
    ["w", "w25", "w75", "w13", "w23", "T", "c", "d", "power", "acc", "h0", "F0"]
    + [x + k for k in "12345" for x in ("h", "F") + SAVED]
    + [x + k for k in "12" for x in ("uu", "uv")]
    + [x + k for k in "345" for x in COTANGENT]
)


def sweep(at, rows, beyond, body):
    beyond = -(-beyond // EDGE) * EDGE
    stop = OWN + rows + beyond
    for start in range(OWN - beyond, stop, STEP):
        n = min(STEP, stop - start)

        def load(name, s=0):
            ref, i = at[name]
            return Pair(*[ref[i, t, start + s : start + s + n, :] for t in range(2)])

        def store(name, value):
            ref, i = at[name]
            ref[i, 0, start : start + n, :] = value.even
            ref[i, 1, start : start + n, :] = value.odd

        body(load, store)


def d_rows(L, name):
    p1, m1, p2, m2 = L(name, 1), L(name, -1), L(name, 2), L(name, -2)
    return 8.0 * (p1 - m1) - (p2 - m2), p1 + m1, p2 + m2


def tend(L, St, k, with_h):
    u, v, H, h = L("u%d" % k), L("v%d" % k), L("H%d" % k), L("h%d" % k)
    xu, su, tu = d_rows(L, "u%d" % k)
    xv, sv, tv = d_rows(L, "v%d" % k)
    yu, ru = d_cols(u)
    yv, rv = d_cols(v)
    near_u = (2.0 * VISC) * (su - 4.0 * u)
    near_v = (2.0 * VISC) * (sv - 4.0 * v)
    ring = Pair(near_u.odd + before(near_u.odd), near_u.even + after(near_u.even))
    bu = (VISC * ((tu + ru) - 12.0 * u) - 4.0 * near_u) + ring
    bv = VISC * ((tv + rv) - 12.0 * v) - 4.0 * near_v
    far = 8.0 * h
    yh = combine(far + near_v, far - near_v, h, h)
    xh = d_rows(L, "h%d" % k)[0]
    q2 = (u * u + v * v) + SPEED_EPS
    rH = H.map(lambda x: 1.0 / x)
    E = L("c") * (q2.map(lax.rsqrt) * rH)
    damp = E * q2
    om = damp.map(lambda x: 1.0 - x)
    for name, value in (
        ("xu", xu), ("xv", xv), ("yu", yu), ("yv", yv), ("dm", damp), ("om", om), ("E", E), ("rH", rH),
    ):
        St(name + str(k), value)
    eu = ((u * xu + v * yu) + xh) + bu
    ev = ((u * xv + v * yv) + yh) + bv
    if not with_h:
        return None, eu, ev, om
    return d_rows(L, "F%d" % k)[0] + d_cols(H * v)[0], eu, ev, om


def moved(L, St, k, with_h):
    eh, eu, ev, om = tend(L, St, k, with_h)
    return (
        L("h%d" % k) - ADV * eh if with_h else None,
        om * L("u%d" % k) - ADV * eu,
        om * L("v%d" % k) - ADV * ev,
    )


def pull(L, k, with_h):
    u, v, H = L("u%d" % k), L("v%d" % k), L("H%d" % k)
    lu, lv = L("lu%d" % k), L("lv%d" % k)
    om, E, rH = L("om%d" % k), L("E%d" % k), L("rH%d" % k)
    xlu, su, tu = d_rows(L, "lu%d" % k)
    _, sv, tv = d_rows(L, "lv%d" % k)
    ylv, rv = d_cols(lv)
    vl = v * lu
    vl8, near, lu_s = 8.0 * vl, (2.0 * VISC) * (su - 4.0 * lu), VISC * lu
    ub = combine(vl8 - near, vl8 + near, vl + lu_s, vl - lu_s)
    ub = ub - (VISC * (tu - 12.0 * lu) - 4.0 * near)
    vl = v * lv
    vl8, near = 8.0 * vl, (2.0 * VISC) * (sv - 4.0 * lv)
    vb = combine(vl8 - near, vl8 + near, vl, vl)
    vb = vb - (VISC * ((tv + rv) - 12.0 * lv) - 4.0 * near)
    ub = ub + d_rows(L, "uu%d" % k)[0] - lu * L("xu%d" % k) - lv * L("xv%d" % k)
    vb = vb + d_rows(L, "uv%d" % k)[0] - lu * L("yu%d" % k) - lv * L("yv%d" % k)
    r = lu * u + lv * v
    rd = r * L("dm%d" % k)
    rE = r * E
    hb = xlu + ylv
    if with_h:
        lh = L("lh%d" % k)
        xlh = d_rows(L, "lh%d" % k)[0]
        ylh = d_cols(lh)[0]
        ub = ub + H * xlh
        vb = vb + H * ylh
        hb = hb + (u * xlh + v * ylh)
    hb = ADV * hb + rd * rH
    if with_h:
        hb = hb + lh
    ub = ADV * ub + (om * lu - rE * u)
    vb = ADV * vb + (om * lv - rE * v)
    return (hb, ub, vb), rd


def step_back(L, s, top):
    new, rd = pull(L, s, True)
    total = []
    for x, value in zip(("lh", "lu", "lv"), new):
        value = value + 3.0 * L(x + str(s + 1))
        if not (top and x == "lh"):
            value = value + 0.5 * L(x + str(s + 2))
        total.append(value)
    return total, rd


def last_kernel(kept_ref, adj_ref, last_ref):
    rows = adj_ref.shape[1]
    at = place_of(KEPT, kept_ref)
    at.update(place_of(["oh", "ou", "ov"], last_ref))

    def body(L, St):
        total, _ = step_back(L, 0, False)
        St("oh", GRAV_RATIO * total[0])
        St("ou", total[1])
        St("ov", total[2])

    sweep(at, rows, 0, body)
    for i in range(3):
        adj_ref[i] = own_columns(rows, [last_ref[i, t, OWN : OWN + rows, :] for t in range(2)])


def spread_matrix():
    shape = (LANES, 2 * LANES)
    hit = lax.broadcasted_iota(jnp.int32, shape, 0) + HALO == column_at(shape, 1)
    return jnp.where(hit, 1.0, 0.0).astype(jnp.bfloat16)


def own_kernel(stack_ref, planes_ref, flags_ref):
    rows = planes_ref.shape[2]
    chosen = spread_matrix()
    for f in range(FIELDS):
        value = pick(thirds(stack_ref[rows * f : rows * (f + 1), :]), chosen)
        for t in range(2):
            planes_ref[f, t] = value[:, LANES * t : LANES * (t + 1)]
    flags_ref[...] = stack_ref[rows * FIELDS :, :]


def main_kernel(counts, own_ref, flags_ref, *rest):
    rows = flags_ref.shape[0] - 8
    rest = list(rest)
    nx, ny = counts
    roles_x = roles("gx", nx)
    row_in = [rest.pop(0) for _ in roles_x]
    sides = 1 if ny == 2 else 2
    side_in = [rest.pop(0) for _ in range(sides)]
    corner_in = [[rest.pop(0) for _ in range(sides)] for _ in roles_x]
    grad_ref, own_sum_ref, other_sum_ref, kept_ref, S = rest
    place_y = lax.axis_index("gy")
    has_left = place_y > 0
    has_right = place_y < ny - 1
    wet = flags_ref[rows : rows + 1, :1]

    at = place_of(PLANES, S)
    at.update(place_of(KEPT, kept_ref))

    def spread(f):
        shape = (LANES, 2 * LANES)
        target = column_at(shape, 1)
        source = lax.broadcasted_iota(jnp.int32, shape, 0)
        blocks = []
        edge = source - HALO * f
        inside = jnp.logical_and(edge >= 0, edge < HALO)
        if sides == 1:
            offset = jnp.where(has_left, 0, LANES + HALO)
            blocks.append(jnp.logical_and(inside, edge + offset == target))
        else:
            hit_left = jnp.logical_and(inside, edge == target)
            hit_right = jnp.logical_and(inside, edge + (LANES + HALO) == target)
            blocks.append(jnp.logical_and(hit_left, has_left))
            blocks.append(jnp.logical_and(hit_right, has_right))
        return jnp.concatenate(
            [jnp.where(b, 1.0, 0.0).astype(jnp.bfloat16) for b in blocks], axis=0
        )

    edge_chosen = [spread(f) for f in range(FIELDS)]
    own_chosen = spread_matrix()

    def put(start, n, centre, edges, wet_centre, exists):
        column = column_at((n, 2 * LANES), 1)
        in_left = column < HALO
        in_right = column >= LANES + HALO
        known = jnp.logical_and(
            jnp.logical_or(jnp.logical_not(in_left), has_left),
            jnp.logical_or(jnp.logical_not(in_right), has_right),
        )
        known = jnp.logical_and(known, column < WIDE)
        if exists is not True:
            known = jnp.logical_and(known, exists)
        edge_parts = [thirds(x) for x in edges]

        edge_parts = [jnp.concatenate([x[i] for x in edge_parts], axis=1) for i in range(3)]

        def extended(f):
            if centre is None:
                value = pick(edge_parts, edge_chosen[f])
                value = value + jnp.concatenate([own_ref[f, 0], own_ref[f, 1]], axis=1)
            else:
                parts = [jnp.concatenate(x, axis=1) for x in zip(thirds(centre(f)), edge_parts)]
                value = pick(parts, jnp.concatenate([own_chosen, edge_chosen[f]], axis=0))
            return jnp.where(known, value, 1.0 if f == 3 else 0.0)

        values = [extended(f) for f in range(FIELDS)]
        wet_left = jnp.broadcast_to(edges[0][:, LANES - 1 :], (n, 2 * LANES))
        wet_right = jnp.broadcast_to(edges[-1][:, LANES - 1 :], (n, 2 * LANES))
        w = jnp.where(in_left, wet_left, jnp.where(in_right, wet_right, wet_centre))
        w = jnp.where(known, w, 0.0)
        h, u, v, d, turb = values
        h, d = GRAV_RATIO * h, GRAV_RATIO * d
        height = d + h
        planes = (
            ("w", w), ("w25", 0.25 * w), ("w75", 0.75 * w), ("w13", (1.0 / 3.0) * w), ("w23", (2.0 / 3.0) * w),
            ("T", turb), ("c", (0.5 * GRAV_RATIO) * (BED_DRAG + turb)), ("d", d),
            ("h0", h), ("u0", u), ("v0", v), ("H0", height), ("F0", height * u),
        )
        for name, value in planes:
            ref, i = at[name]
            for t in range(2):
                ref[i, t, pl.ds(start, n), :] = value[:, LANES * t : LANES * (t + 1)]

    put(OWN, rows, None, [x[...] for x in side_in], jnp.broadcast_to(wet, (rows, 2 * LANES)), True)
    for (partner_after, exists), rin, corners in zip(roles_x, row_in, corner_in):
        put(
            pl.multiple_of(GUARD + partner_after * (rows + HALO), 8),
            HALO,
            lambda f: rin[HALO * f : HALO * (f + 1), :],
            [x[...] for x in corners],
            jnp.broadcast_to(rin[LANES - 1 :, :1], (HALO, 2 * LANES)),
            exists,
        )

    def keep_state(L, St, k, h, u, v):
        H = L("d") + h
        St("h%d" % k, h)
        St("u%d" % k, u)
        St("v%d" % k, v)
        St("H%d" % k, H)
        St("F%d" % k, H * u)

    for n in range(2):
        s, a, b = 3 * n, 3 * n + 1, 3 * n + 2

        def first(L, St):
            w = L("w")
            keep_state(L, St, a, *[w * x for x in moved(L, St, s, True)])

        sweep(at, rows, HALO - 2 - 2 * s, first)

        def second(L, St):
            old, new = L("w75"), L("w25")
            state = [L(x + str(s)) for x in "huv"]
            keep_state(L, St, b, *[old * x + new * y for x, y in zip(state, moved(L, St, a, True))])

        sweep(at, rows, HALO - 2 - 2 * a, second)

        def third(L, St):
            old, new = L("w13"), L("w23")
            h, u, v = moved(L, St, b, n == 0)
            u = old * L("u%d" % s) + new * u
            v = old * L("v%d" % s) + new * v
            if n == 0:
                keep_state(L, St, 3, old * L("h0") + new * h, u, v)
                return
            q2 = (u * u + v * v) + SPEED_EPS
            q = q2.map(jnp.sqrt)
            w = L("w")
            St("power", w * (q2 * q))
            fac = (3.0 * new) * (L("T") * w * q)
            lu, lv = fac * u, fac * v
            ub = L("u5")
            St("lu5", lu)
            St("lv5", lv)
            St("uu5", ub * lu)
            St("uv5", ub * lv)

        sweep(at, rows, HALO - 2 - 2 * b, third)

    def keep_cot(L, St, k, lh, lu, lv):
        u = L("u%d" % k)
        St("lh%d" % k, lh)
        St("lu%d" % k, lu)
        St("lv%d" % k, lv)
        St("uu%d" % k, u * lu)
        St("uv%d" % k, u * lv)

    for n in (1, 0):
        s, a, b = 3 * n, 3 * n + 1, 3 * n + 2
        top = n == 1

        def from_b(L, St):
            new, rd = pull(L, b, not top)
            St("acc", rd if top else L("acc") + rd)
            quarter = L("w25")
            keep_cot(L, St, a, *[quarter * x for x in new])

        sweep(at, rows, 2 * b, from_b)

        def from_a(L, St):
            new, rd = pull(L, a, True)
            w = L("w")
            lh, lu, lv = [w * x for x in new]
            if not top:
                rd = rd + (lu * L("u0") + lv * L("v0")) * L("dm0")
            St("acc", L("acc") + rd)
            keep_cot(L, St, s, lh, lu, lv)

        sweep(at, rows, 2 * a, from_a)

        def from_s(L, St):
            total, rd = step_back(L, s, True)
            St("acc", L("acc") + rd)
            scale = L("w23")
            keep_cot(L, St, 2, *[scale * x for x in total])

        if top:
            sweep(at, rows, 2 * s, from_s)

    def own_rows(name):
        ref, i = at[name]
        return [ref[i, t, OWN : OWN + rows, :] for t in range(2)]

    share = [
        p - a / (BED_DRAG + t) for p, a, t in zip(own_rows("power"), own_rows("acc"), own_rows("T"))
    ]
    grad = own_columns(rows, share)
    grad_ref[...] = grad
    matched = flags_ref[:rows, :] > 0.5
    scale = 1.0 / (rows * LANES)
    for ref, part in ((own_sum_ref, jnp.where(matched, grad, 0.0)), (other_sum_ref, jnp.where(matched, 0.0, grad))):
        total = jnp.sum(jnp.sum(part, axis=0, keepdims=True), axis=1, keepdims=True) * scale
        ref[...] = jnp.broadcast_to(total, (1, LANES))


def shards(elevation, velocity, depth, turbine, wet_tiles, farm):
    rows = elevation.shape[0]
    counts = (lax.axis_size("gx"), lax.axis_size("gy"))
    nx, ny = counts
    elev = elevation.reshape(rows, LANES)
    vel = velocity.reshape(2, rows, LANES)
    dep = depth.reshape(rows, LANES)
    turb = turbine.reshape(rows, LANES)
    farm_local = farm.reshape(rows, LANES)
    pairs_x = pairings(nx)
    pairs_y = pairings(ny)
    f32 = jnp.float32
    square = jax.ShapeDtypeStruct((LANES, LANES), f32)
    side = jax.ShapeDtypeStruct((rows, LANES), f32)
    corner = jax.ShapeDtypeStruct((HALO, LANES), f32)
    vmem = pl.BlockSpec(memory_space=pltpu.VMEM)
    shapes = [square] * len(pairs_x) + [side] * len(pairs_y) + [corner] * (len(pairs_x) * len(pairs_y))
    shapes.append(jax.ShapeDtypeStruct((rows * (FIELDS + 1) + 8, LANES), f32))
    sent = pl.pallas_call(
        lambda *refs: pack_kernel(counts, *refs),
        out_shape=shapes,
        in_specs=[vmem] * 6,
        out_specs=[vmem] * len(shapes),
        name="pack",
    )(wet_tiles, elev, vel, dep, turb, farm_local)
    sent = list(sent)
    stack = sent.pop()
    row_got = [lax.ppermute(sent.pop(0), "gx", list(enumerate(p))) for p in pairs_x]
    side_got = [lax.ppermute(sent.pop(0), "gy", list(enumerate(p))) for p in pairs_y]
    corner_got = [
        [
            lax.ppermute(
                sent.pop(0),
                ("gx", "gy"),
                [(i * ny + j, px[i] * ny + py[j]) for i in range(nx) for j in range(ny)],
            )
            for py in pairs_y
        ]
        for px in pairs_x
    ]

    def left_right(got):
        if len(got) == 1:
            return got
        odd = lax.rem(lax.axis_index("gy"), 2) == 1
        return [jnp.where(odd, got[0], got[1]), jnp.where(odd, got[1], got[0])]

    edges = left_right(side_got)
    corners = [c for got in corner_got for c in left_right(got)]
    own_planes, flags = pl.pallas_call(
        own_kernel,
        out_shape=[
            jax.ShapeDtypeStruct((FIELDS, 2, rows, LANES), f32),
            jax.ShapeDtypeStruct((rows + 8, LANES), f32),
        ],
        in_specs=[vmem],
        out_specs=[vmem] * 2,
        compiler_params=pltpu.CompilerParams(vmem_limit_bytes=VMEM_OWN),
        cost_estimate=pl.CostEstimate(flops=4000000, bytes_accessed=6000000, transcendentals=0),
        name="own",
    )(stack)
    n_in = 2 + len(row_got) + len(edges) + len(corners)
    plane = (2, rows + 2 * OWN, LANES)
    grad, own_sum, other_sum, kept = pl.pallas_call(
        lambda *refs: main_kernel(counts, *refs),
        out_shape=[
            side,
            jax.ShapeDtypeStruct((1, LANES), f32),
            jax.ShapeDtypeStruct((1, LANES), f32),
            jax.ShapeDtypeStruct((len(KEPT),) + plane, f32),
        ],
        in_specs=[vmem] * n_in,
        out_specs=[vmem] * 4,
        scratch_shapes=[pltpu.VMEM((len(PLANES),) + plane, f32)],
        compiler_params=pltpu.CompilerParams(vmem_limit_bytes=VMEM_MAIN),
        name="adjoint",
    )(own_planes, flags, *row_got, *edges, *corners)
    passed = lax.ppermute(other_sum, "gx", [(i, (i + 1) % nx) for i in range(nx)])
    adjoint = pl.pallas_call(
        last_kernel,
        out_shape=jax.ShapeDtypeStruct((3, rows, LANES), f32),
        in_specs=[vmem],
        out_specs=vmem,
        scratch_shapes=[pltpu.VMEM((3,) + plane, f32)],
        compiler_params=pltpu.CompilerParams(vmem_limit_bytes=VMEM_LAST),
        cost_estimate=pl.CostEstimate(flops=4000000, bytes_accessed=6000000, transcendentals=0),
        name="last",
    )(kept)
    return (
        adjoint.reshape((3,) + elevation.shape),
        grad.reshape(elevation.shape),
        (own_sum + passed)[0, :1],
    )


def solution(mesh):
    in_specs = (
        P("gx", None, "gy", None),
        P(None, "gx", None, "gy", None),
        P("gx", None, "gy", None),
        P("gx", None, "gy", None),
        P("gx", None, "gy"),
        P("gx", None, "gy", None),
    )
    out_specs = (P(None, "gx", None, "gy", None), P("gx", None, "gy", None), P(("gx", "gy")))
    return jax.shard_map(shards, mesh=mesh, in_specs=in_specs, out_specs=out_specs, check_vma=False)
```

time: 29.9 us -> 28.7 us (0.960)
  waiting for transfers between devices: 7.75 us -> 4.67 us
  Pallas kernels: 11.7 us -> 12.8 us
  local copies, waits for them, and re-layouts: 0.02 us -> 1 us
    ppermute x1, waiting for transfers between devices: 5.36 us -> 3.7 us  [shards(): lax.ppermute(other_sum, 'gx', [(i, (i + 1) % nx) for i in range(nx)])]
    ppermute x2, waiting for transfers between devices: 2.39 us -> 0.96 us  [shards(): lax.ppermute(sent.pop(0), ('gx', 'gy'), [(i * ny + j, px[i] * ny + py[j])...]
    pallas_call x1 -> x3, Pallas kernels: 9.82 us -> 10.8 us  [the longest x1 8.73 us: shards(): pl.pallas_call(lambda *refs: main_kernel(counts, *refs), out_shape=[side,...]
    unnamed x12 -> x2, local copies, waits for them, and re-layouts: 0.02 us -> 1 us
  transfers between devices with their start and end apart: 6 -> 6, of which waited for: 3 -> 2; matrix products, arithmetic and copies ran while one was open for 0% -> 0% of each run, Pallas kernels for 0% -> 7%
where the time goes in v3:
time: 28.7 us; the launch traced here: 28.5 us
  Pallas kernels  12.8 us (45%)
  starting transfers between devices  8.2 us (29%)
  waiting for transfers between devices  4.67 us (16%)
  between operations  1.3 us (5%)
  local copies, waits for them, and re-layouts  1 us (3%)
  other arithmetic  0.51 us (2%)
    pallas_call x1, Pallas kernels, shards(): pl.pallas_call(lambda *refs: main_kernel(counts, *refs), out_shape=[side,...  8.73 us
    ppermute x1, waiting for transfers between devices, shards(): lax.ppermute(other_sum, 'gx', [(i, (i + 1) % nx) for i in range(nx)])  3.7 us
    ppermute x2, starting transfers between devices, shards(): lax.ppermute(sent.pop(0), ('gx', 'gy'), [(i * ny + j, px[i] * ny + py[j])...  3.44 us
    ppermute x1, starting transfers between devices, shards(): lax.ppermute(sent.pop(0), 'gy', list(enumerate(p)))  2.53 us
    pallas_call x1, Pallas kernels, shards(): pl.pallas_call(lambda *refs: pack_kernel(counts, *refs), out_shape=shapes...  1.97 us
    ppermute x2, starting transfers between devices, shards(): lax.ppermute(sent.pop(0), 'gx', list(enumerate(p)))  1.94 us
    pallas_call x1, Pallas kernels, shards(): pl.pallas_call(last_kernel, out_shape=jax.ShapeDtypeStruct((3, rows, LANE...  1.67 us
    unnamed x2, local copies, waits for them, and re-layouts  1 us
  transfers between devices with their start and end apart: 6, of which 2 were waited for; matrix products, arithmetic and copies ran while one was open for 0% of the time, Pallas kernels for 7%

profile of v3, /device:TPU:0, one launch (start us, length us, event | category | flops | bytes accessed | tf_op | source)
XLA Modules:
  0.0 28.5 jit_solution(7966522462227300192)
XLA Ops:
  1.3 2.0 %pack.1 = (f32[128,128]{1,0:T(8,128)}, f32[128,128]{1,0:T(8,128)}, f32[128,128]{1,0:T(8,128)}, f32[24,128]{1,0:T(8,128)}, f32[24,128]{1,0:T(8,128)}, /*index=5*/f32[776,128]{1,0:T(8,128)}) custom-call(s32[1,1,1]{2,1,0:T(1,128)S(6)} %copy.11.refs_0_, f32[128,128]{1,0:T(8,128)} %bitcast.15, f32[2,128,128]{2,1,0:T(8,128)} %bitcast.14, f32[128,128]{1,0:T(8,128)} %bitcast.16, ...), custom_call_target="tpu_custom_call" | custom-call | tf_op jit(solution)/shard_map/pack/pallas_call | solution.py:533
  3.2 0.5 %collective-permute-start = (f32[128,128]{1,0:T(8,128)}, f32[128,128]{1,0:T(8,128)S(1)}, u32[]{:S(2)}, u32[]{:S(2)}) collective-permute-start(f32[128,128]{1,0:T(8,128)} %get-tuple-element.18), channel_id=1, source_target_pairs={{0,2},{2,0},{4,6},{6,4},{8,10},{10,8},{12,14},{14,12},{16,18},{18,... | collective-permute-start | bytes 196616 | tf_op jit(solution)/shard_map/ppermute | solution.py:542
  3.7 1.5 %collective-permute-start.1 = (f32[128,128]{1,0:T(8,128)}, f32[128,128]{1,0:T(8,128)S(1)}, u32[]{:S(2)}, u32[]{:S(2)}) collective-permute-start(f32[128,128]{1,0:T(8,128)} %get-tuple-element.19), channel_id=1, source_target_pairs={{0,0},{2,4},{4,2},{6,8},{8,6},{10,12},{12,10},{14,16},{16,14},{18,... | collective-permute-start | bytes 196616 | tf_op jit(solution)/shard_map/ppermute | solution.py:542
  5.2 2.5 %collective-permute-start.2 = (f32[128,128]{1,0:T(8,128)}, f32[128,128]{1,0:T(8,128)S(1)}, u32[]{:S(2)}, u32[]{:S(2)}) collective-permute-start(f32[128,128]{1,0:T(8,128)} %get-tuple-element.20), channel_id=1, source_target_pairs={{0,1},{1,0},{2,3},{3,2},{4,5},{5,4},{6,7},{7,6},{8,9},{9,8},{10,11... | collective-permute-start | bytes 196616 | tf_op jit(solution)/shard_map/ppermute | solution.py:543
  7.7 1.9 %collective-permute-start.3 = (f32[24,128]{1,0:T(8,128)}, f32[24,128]{1,0:T(8,128)S(1)}, u32[]{:S(2)}, u32[]{:S(2)}) collective-permute-start(f32[24,128]{1,0:T(8,128)} %get-tuple-element.21), channel_id=1, source_target_pairs={{0,3},{1,2},{2,1},{3,0},{4,7},{5,6},{6,5},{7,4},{8,11},{9,10},{10,... | collective-permute-start | bytes 36872 | tf_op jit(solution)/shard_map/ppermute | solution.py:546
  9.6 1.5 %collective-permute-start.4 = (f32[24,128]{1,0:T(8,128)}, f32[24,128]{1,0:T(8,128)S(1)}, u32[]{:S(2)}, u32[]{:S(2)}) collective-permute-start(f32[24,128]{1,0:T(8,128)} %get-tuple-element.22), channel_id=1, source_target_pairs={{0,1},{1,0},{2,5},{3,4},{4,3},{5,2},{6,9},{7,8},{8,7},{9,6},{10,13... | collective-permute-start | bytes 36872 | tf_op jit(solution)/shard_map/ppermute | solution.py:546
  11.2 0.0 copy-start
  11.2 1.0 %copy-done = f32[776,128]{1,0:T(8,128)S(1)} copy-done((f32[776,128]{1,0:T(8,128)S(1)}, f32[776,128]{1,0:T(8,128)}, u32[]{:S(2)}) %copy-start) | copy-done | bytes 397336
  12.2 0.4 %own.1 = (f32[5,2,128,128]{3,2,1,0:T(8,128)S(1)}, f32[136,128]{1,0:T(8,128)S(1)}) custom-call(f32[776,128]{1,0:T(8,128)S(1)} %copy-done), custom_call_target="tpu_custom_call" | custom-call | flops 4000000 | bytes 6000000 | tf_op jit(solution)/shard_map/own/pallas_call | solution.py:564
  12.6 0.0 collective-permute-done.3.refs_5_
  12.6 1.0 %collective-permute-done.4.refs_6_ = f32[24,128]{1,0:T(8,128)S(1)} collective-permute-done((f32[24,128]{1,0:T(8,128)}, f32[24,128]{1,0:T(8,128)S(1)}, u32[]{:S(2)}, u32[]{:S(2)}) %collective-permute-start.4) | collective-permute-done | bytes 12320 | tf_op jit(solution)/shard_map/ppermute | solution.py:546
  13.5 0.0 collective-permute-done.refs_2_
  13.5 0.0 collective-permute-done.1.refs_3_
  13.6 0.0 collective-permute-done.2.refs_4_
  13.6 8.7 %adjoint.1 = (f32[128,128]{1,0:T(8,128)}, f32[1,128]{1,0:T(1,128)S(1)}, f32[1,128]{1,0:T(1,128)S(1)}, f32[22,2,192,128]{3,2,1,0:T(8,128)S(1)}) custom-call(f32[5,2,128,128]{3,2,1,0:T(8,128)S(1)} %get-tuple-element.16.refs_0_, f32[136,128]{1,0:T(8,128)S(1)} %get-tuple-element.17.refs_1_, f32[128,128]{1,0:T(8,128)S(1)} %collective-permute-done.refs_2_, ...), custom_call_target="tpu_custom_call" | custom-call | tf_op jit(solution)/shard_map/adjoint/pallas_call | solution.py:578
  22.3 0.3 %collective-permute-start.5 = (f32[1,128]{1,0:T(1,128)S(1)}, f32[1,128]{1,0:T(1,128)S(1)}, u32[]{:S(2)}, u32[]{:S(2)}) collective-permute-start(f32[1,128]{1,0:T(1,128)S(1)} %get-tuple-element.26), channel_id=1, source_target_pairs={{0,2},{2,4},{4,6},{6,8},{8,10},{10,12},{12,14},{14,16},{16,18},{18... | collective-permute-start | bytes 1544 | tf_op jit(solution)/shard_map/ppermute | solution.py:592
  22.6 1.7 %last.1 = f32[3,128,128]{2,1,0:T(8,128)} custom-call(f32[22,2,192,128]{3,2,1,0:T(8,128)S(1)} %get-tuple-element.23.kept_ref), custom_call_target="tpu_custom_call" | custom-call | flops 4000000 | bytes 6000000 | tf_op jit(solution)/shard_map/last/pallas_call | solution.py:593
  24.3 3.7 %collective-permute-done.5 = f32[1,128]{1,0:T(1,128)S(1)} collective-permute-done((f32[1,128]{1,0:T(1,128)S(1)}, f32[1,128]{1,0:T(1,128)S(1)}, u32[]{:S(2)}, u32[]{:S(2)}) %collective-permute-start.5) | collective-permute-done | bytes 544 | tf_op jit(solution)/shard_map/ppermute | solution.py:592
  27.9 0.5 %add.3 = f32[1,128]{1,0:T(1,128)} add(f32[1,128]{1,0:T(1,128)S(1)} %get-tuple-element.25, f32[1,128]{1,0:T(1,128)S(1)} %collective-permute-done.5) | non-fusion elementwise | flops 128 | bytes 1536 | tf_op jit(solution)/shard_map/add | solution.py:606
Async XLA Ops:
  3.2 10.3 %collective-permute-start = (f32[128,128]{1,0:T(8,128)}, f32[128,128]{1,0:T(8,128)S(1)}, u32[]{:S(2)}, u32[]{:S(2)}) collective-permute-start(f32[128,128]{1,0:T(8,128)} %get-tuple-element.18), channel_id=1, source_target_pairs={{0,2},{2,0},{4,6},{6,4},{8,10},{10,8},{12,14},{14,12},{16,18},{18,... | collective-permute-start | bytes 196616 | tf_op jit(solution)/shard_map/ppermute | solution.py:542
  3.7 9.9 %collective-permute-start.1 = (f32[128,128]{1,0:T(8,128)}, f32[128,128]{1,0:T(8,128)S(1)}, u32[]{:S(2)}, u32[]{:S(2)}) collective-permute-start(f32[128,128]{1,0:T(8,128)} %get-tuple-element.19), channel_id=1, source_target_pairs={{0,0},{2,4},{4,2},{6,8},{8,6},{10,12},{12,10},{14,16},{16,14},{18,... | collective-permute-start | bytes 196616 | tf_op jit(solution)/shard_map/ppermute | solution.py:542
  5.2 8.4 %collective-permute-start.2 = (f32[128,128]{1,0:T(8,128)}, f32[128,128]{1,0:T(8,128)S(1)}, u32[]{:S(2)}, u32[]{:S(2)}) collective-permute-start(f32[128,128]{1,0:T(8,128)} %get-tuple-element.20), channel_id=1, source_target_pairs={{0,1},{1,0},{2,3},{3,2},{4,5},{5,4},{6,7},{7,6},{8,9},{9,8},{10,11... | collective-permute-start | bytes 196616 | tf_op jit(solution)/shard_map/ppermute | solution.py:543
  7.7 4.9 %collective-permute-start.3 = (f32[24,128]{1,0:T(8,128)}, f32[24,128]{1,0:T(8,128)S(1)}, u32[]{:S(2)}, u32[]{:S(2)}) collective-permute-start(f32[24,128]{1,0:T(8,128)} %get-tuple-element.21), channel_id=1, source_target_pairs={{0,3},{1,2},{2,1},{3,0},{4,7},{5,6},{6,5},{7,4},{8,11},{9,10},{10,... | collective-permute-start | bytes 36872 | tf_op jit(solution)/shard_map/ppermute | solution.py:546
  9.6 3.9 %collective-permute-start.4 = (f32[24,128]{1,0:T(8,128)}, f32[24,128]{1,0:T(8,128)S(1)}, u32[]{:S(2)}, u32[]{:S(2)}) collective-permute-start(f32[24,128]{1,0:T(8,128)} %get-tuple-element.22), channel_id=1, source_target_pairs={{0,1},{1,0},{2,5},{3,4},{4,3},{5,2},{6,9},{7,8},{8,7},{9,6},{10,13... | collective-permute-start | bytes 36872 | tf_op jit(solution)/shard_map/ppermute | solution.py:546
  11.2 1.0 %copy-start = (f32[776,128]{1,0:T(8,128)S(1)}, f32[776,128]{1,0:T(8,128)}, u32[]{:S(2)}) copy-start(f32[776,128]{1,0:T(8,128)} %get-tuple-element.15.stack_ref) | copy-start | bytes 1191940
  22.3 5.7 %collective-permute-start.5 = (f32[1,128]{1,0:T(1,128)S(1)}, f32[1,128]{1,0:T(1,128)S(1)}, u32[]{:S(2)}, u32[]{:S(2)}) collective-permute-start(f32[1,128]{1,0:T(1,128)S(1)} %get-tuple-element.26), channel_id=1, source_target_pairs={{0,2},{2,4},{4,6},{6,8},{8,10},{10,12},{12,14},{14,16},{16,18},{18... | collective-permute-start | bytes 1544 | tf_op jit(solution)/shard_map/ppermute | solution.py:592

commit v4 on v3

--- a/solution.py
+++ b/solution.py
@@ -68,11 +68,7 @@
     for (after, _), out in zip(roles_y, side_outs):
         packed = jnp.broadcast_to(wet, (rows, LANES))
         for f in reversed(range(FIELDS)):
-            moved = jnp.where(
-                after == 1,
-                pltpu.roll(fields[f], HALO * (f + 1), 1),
-                pltpu.roll(fields[f], HALO * f, 1),
-            )
+            moved = pltpu.roll(fields[f], HALO * (f + after), 1)
             packed = jnp.where(lane < HALO * (f + 1), moved, packed)
         out[...] = packed
     for start in starts:

time: 28.7 us -> 28.6 us (level)
  no operation moved by 1% of the time
where the time goes in v4:
time: 28.6 us; the launch traced here: 28.4 us
  Pallas kernels  12.7 us (44%)
  starting transfers between devices  8.2 us (29%)
  waiting for transfers between devices  4.67 us (16%)
  between operations  1.3 us (5%)
  local copies, waits for them, and re-layouts  1 us (3%)
  other arithmetic  0.51 us (2%)
    pallas_call x1, Pallas kernels, shards(): pl.pallas_call(lambda *refs: main_kernel(counts, *refs), out_shape=[side,...  8.73 us
    ppermute x1, waiting for transfers between devices, shards(): lax.ppermute(other_sum, 'gx', [(i, (i + 1) % nx) for i in range(nx)])  3.7 us
    ppermute x2, starting transfers between devices, shards(): lax.ppermute(sent.pop(0), ('gx', 'gy'), [(i * ny + j, px[i] * ny + py[j])...  3.44 us
    ppermute x1, starting transfers between devices, shards(): lax.ppermute(sent.pop(0), 'gy', list(enumerate(p)))  2.53 us
    ppermute x2, starting transfers between devices, shards(): lax.ppermute(sent.pop(0), 'gx', list(enumerate(p)))  1.94 us
    pallas_call x1, Pallas kernels, shards(): pl.pallas_call(lambda *refs: pack_kernel(counts, *refs), out_shape=shapes...  1.9 us
    pallas_call x1, Pallas kernels, shards(): pl.pallas_call(last_kernel, out_shape=jax.ShapeDtypeStruct((3, rows, LANE...  1.67 us
    unnamed x2, local copies, waits for them, and re-layouts  1 us
  transfers between devices with their start and end apart: 6, of which 2 were waited for; matrix products, arithmetic and copies ran while one was open for 0% of the time, Pallas kernels for 7%

profile of v4, /device:TPU:0, one launch (start us, length us, event | category | flops | bytes accessed | tf_op | source)
XLA Modules:
  0.0 28.4 jit_solution(12820285391408676666)
XLA Ops:
  1.3 1.9 %pack.1 = (f32[128,128]{1,0:T(8,128)}, f32[128,128]{1,0:T(8,128)}, f32[128,128]{1,0:T(8,128)}, f32[24,128]{1,0:T(8,128)}, f32[24,128]{1,0:T(8,128)}, /*index=5*/f32[776,128]{1,0:T(8,128)}) custom-call(s32[1,1,1]{2,1,0:T(1,128)S(6)} %copy.11.refs_0_, f32[128,128]{1,0:T(8,128)} %bitcast.15, f32[2,128,128]{2,1,0:T(8,128)} %bitcast.14, f32[128,128]{1,0:T(8,128)} %bitcast.16, ...), custom_call_target="tpu_custom_call" | custom-call | tf_op jit(solution)/shard_map/pack/pallas_call | solution.py:529
  3.2 0.5 %collective-permute-start = (f32[128,128]{1,0:T(8,128)}, f32[128,128]{1,0:T(8,128)S(1)}, u32[]{:S(2)}, u32[]{:S(2)}) collective-permute-start(f32[128,128]{1,0:T(8,128)} %get-tuple-element.18), channel_id=1, source_target_pairs={{0,2},{2,0},{4,6},{6,4},{8,10},{10,8},{12,14},{14,12},{16,18},{18,... | collective-permute-start | bytes 196616 | tf_op jit(solution)/shard_map/ppermute | solution.py:538
  3.6 1.5 %collective-permute-start.1 = (f32[128,128]{1,0:T(8,128)}, f32[128,128]{1,0:T(8,128)S(1)}, u32[]{:S(2)}, u32[]{:S(2)}) collective-permute-start(f32[128,128]{1,0:T(8,128)} %get-tuple-element.19), channel_id=1, source_target_pairs={{0,0},{2,4},{4,2},{6,8},{8,6},{10,12},{12,10},{14,16},{16,14},{18,... | collective-permute-start | bytes 196616 | tf_op jit(solution)/shard_map/ppermute | solution.py:538
  5.1 2.5 %collective-permute-start.2 = (f32[128,128]{1,0:T(8,128)}, f32[128,128]{1,0:T(8,128)S(1)}, u32[]{:S(2)}, u32[]{:S(2)}) collective-permute-start(f32[128,128]{1,0:T(8,128)} %get-tuple-element.20), channel_id=1, source_target_pairs={{0,1},{1,0},{2,3},{3,2},{4,5},{5,4},{6,7},{7,6},{8,9},{9,8},{10,11... | collective-permute-start | bytes 196616 | tf_op jit(solution)/shard_map/ppermute | solution.py:539
  7.7 1.9 %collective-permute-start.3 = (f32[24,128]{1,0:T(8,128)}, f32[24,128]{1,0:T(8,128)S(1)}, u32[]{:S(2)}, u32[]{:S(2)}) collective-permute-start(f32[24,128]{1,0:T(8,128)} %get-tuple-element.21), channel_id=1, source_target_pairs={{0,3},{1,2},{2,1},{3,0},{4,7},{5,6},{6,5},{7,4},{8,11},{9,10},{10,... | collective-permute-start | bytes 36872 | tf_op jit(solution)/shard_map/ppermute | solution.py:542
  9.6 1.5 %collective-permute-start.4 = (f32[24,128]{1,0:T(8,128)}, f32[24,128]{1,0:T(8,128)S(1)}, u32[]{:S(2)}, u32[]{:S(2)}) collective-permute-start(f32[24,128]{1,0:T(8,128)} %get-tuple-element.22), channel_id=1, source_target_pairs={{0,1},{1,0},{2,5},{3,4},{4,3},{5,2},{6,9},{7,8},{8,7},{9,6},{10,13... | collective-permute-start | bytes 36872 | tf_op jit(solution)/shard_map/ppermute | solution.py:542
  11.1 0.0 copy-start
  11.1 1.0 %copy-done = f32[776,128]{1,0:T(8,128)S(1)} copy-done((f32[776,128]{1,0:T(8,128)S(1)}, f32[776,128]{1,0:T(8,128)}, u32[]{:S(2)}) %copy-start) | copy-done | bytes 397336
  12.1 0.4 %own.1 = (f32[5,2,128,128]{3,2,1,0:T(8,128)S(1)}, f32[136,128]{1,0:T(8,128)S(1)}) custom-call(f32[776,128]{1,0:T(8,128)S(1)} %copy-done), custom_call_target="tpu_custom_call" | custom-call | flops 4000000 | bytes 6000000 | tf_op jit(solution)/shard_map/own/pallas_call | solution.py:560
  12.5 0.0 collective-permute-done.3.refs_5_
  12.5 1.0 %collective-permute-done.4.refs_6_ = f32[24,128]{1,0:T(8,128)S(1)} collective-permute-done((f32[24,128]{1,0:T(8,128)}, f32[24,128]{1,0:T(8,128)S(1)}, u32[]{:S(2)}, u32[]{:S(2)}) %collective-permute-start.4) | collective-permute-done | bytes 12320 | tf_op jit(solution)/shard_map/ppermute | solution.py:542
  13.5 0.0 collective-permute-done.refs_2_
  13.5 0.0 collective-permute-done.1.refs_3_
  13.5 0.0 collective-permute-done.2.refs_4_
  13.5 8.7 %adjoint.1 = (f32[128,128]{1,0:T(8,128)}, f32[1,128]{1,0:T(1,128)S(1)}, f32[1,128]{1,0:T(1,128)S(1)}, f32[22,2,192,128]{3,2,1,0:T(8,128)S(1)}) custom-call(f32[5,2,128,128]{3,2,1,0:T(8,128)S(1)} %get-tuple-element.16.refs_0_, f32[136,128]{1,0:T(8,128)S(1)} %get-tuple-element.17.refs_1_, f32[128,128]{1,0:T(8,128)S(1)} %collective-permute-done.refs_2_, ...), custom_call_target="tpu_custom_call" | custom-call | tf_op jit(solution)/shard_map/adjoint/pallas_call | solution.py:574
  22.2 0.3 %collective-permute-start.5 = (f32[1,128]{1,0:T(1,128)S(1)}, f32[1,128]{1,0:T(1,128)S(1)}, u32[]{:S(2)}, u32[]{:S(2)}) collective-permute-start(f32[1,128]{1,0:T(1,128)S(1)} %get-tuple-element.26), channel_id=1, source_target_pairs={{0,2},{2,4},{4,6},{6,8},{8,10},{10,12},{12,14},{14,16},{16,18},{18... | collective-permute-start | bytes 1544 | tf_op jit(solution)/shard_map/ppermute | solution.py:588
  22.5 1.7 %last.1 = f32[3,128,128]{2,1,0:T(8,128)} custom-call(f32[22,2,192,128]{3,2,1,0:T(8,128)S(1)} %get-tuple-element.23.kept_ref), custom_call_target="tpu_custom_call" | custom-call | flops 4000000 | bytes 6000000 | tf_op jit(solution)/shard_map/last/pallas_call | solution.py:589
  24.2 3.7 %collective-permute-done.5 = f32[1,128]{1,0:T(1,128)S(1)} collective-permute-done((f32[1,128]{1,0:T(1,128)S(1)}, f32[1,128]{1,0:T(1,128)S(1)}, u32[]{:S(2)}, u32[]{:S(2)}) %collective-permute-start.5) | collective-permute-done | bytes 544 | tf_op jit(solution)/shard_map/ppermute | solution.py:588
  27.9 0.5 %add.3 = f32[1,128]{1,0:T(1,128)} add(f32[1,128]{1,0:T(1,128)S(1)} %get-tuple-element.25, f32[1,128]{1,0:T(1,128)S(1)} %collective-permute-done.5) | non-fusion elementwise | flops 128 | bytes 1536 | tf_op jit(solution)/shard_map/add | solution.py:602
Async XLA Ops:
  3.2 10.3 %collective-permute-start = (f32[128,128]{1,0:T(8,128)}, f32[128,128]{1,0:T(8,128)S(1)}, u32[]{:S(2)}, u32[]{:S(2)}) collective-permute-start(f32[128,128]{1,0:T(8,128)} %get-tuple-element.18), channel_id=1, source_target_pairs={{0,2},{2,0},{4,6},{6,4},{8,10},{10,8},{12,14},{14,12},{16,18},{18,... | collective-permute-start | bytes 196616 | tf_op jit(solution)/shard_map/ppermute | solution.py:538
  3.6 9.9 %collective-permute-start.1 = (f32[128,128]{1,0:T(8,128)}, f32[128,128]{1,0:T(8,128)S(1)}, u32[]{:S(2)}, u32[]{:S(2)}) collective-permute-start(f32[128,128]{1,0:T(8,128)} %get-tuple-element.19), channel_id=1, source_target_pairs={{0,0},{2,4},{4,2},{6,8},{8,6},{10,12},{12,10},{14,16},{16,14},{18,... | collective-permute-start | bytes 196616 | tf_op jit(solution)/shard_map/ppermute | solution.py:538
  5.1 8.4 %collective-permute-start.2 = (f32[128,128]{1,0:T(8,128)}, f32[128,128]{1,0:T(8,128)S(1)}, u32[]{:S(2)}, u32[]{:S(2)}) collective-permute-start(f32[128,128]{1,0:T(8,128)} %get-tuple-element.20), channel_id=1, source_target_pairs={{0,1},{1,0},{2,3},{3,2},{4,5},{5,4},{6,7},{7,6},{8,9},{9,8},{10,11... | collective-permute-start | bytes 196616 | tf_op jit(solution)/shard_map/ppermute | solution.py:539
  7.7 4.9 %collective-permute-start.3 = (f32[24,128]{1,0:T(8,128)}, f32[24,128]{1,0:T(8,128)S(1)}, u32[]{:S(2)}, u32[]{:S(2)}) collective-permute-start(f32[24,128]{1,0:T(8,128)} %get-tuple-element.21), channel_id=1, source_target_pairs={{0,3},{1,2},{2,1},{3,0},{4,7},{5,6},{6,5},{7,4},{8,11},{9,10},{10,... | collective-permute-start | bytes 36872 | tf_op jit(solution)/shard_map/ppermute | solution.py:542
  9.6 3.9 %collective-permute-start.4 = (f32[24,128]{1,0:T(8,128)}, f32[24,128]{1,0:T(8,128)S(1)}, u32[]{:S(2)}, u32[]{:S(2)}) collective-permute-start(f32[24,128]{1,0:T(8,128)} %get-tuple-element.22), channel_id=1, source_target_pairs={{0,1},{1,0},{2,5},{3,4},{4,3},{5,2},{6,9},{7,8},{8,7},{9,6},{10,13... | collective-permute-start | bytes 36872 | tf_op jit(solution)/shard_map/ppermute | solution.py:542
  11.1 1.0 %copy-start = (f32[776,128]{1,0:T(8,128)S(1)}, f32[776,128]{1,0:T(8,128)}, u32[]{:S(2)}) copy-start(f32[776,128]{1,0:T(8,128)} %get-tuple-element.15.stack_ref) | copy-start | bytes 1191940
  22.2 5.7 %collective-permute-start.5 = (f32[1,128]{1,0:T(1,128)S(1)}, f32[1,128]{1,0:T(1,128)S(1)}, u32[]{:S(2)}, u32[]{:S(2)}) collective-permute-start(f32[1,128]{1,0:T(1,128)S(1)} %get-tuple-element.26), channel_id=1, source_target_pairs={{0,2},{2,4},{4,6},{6,8},{8,10},{10,12},{12,14},{14,16},{16,18},{18... | collective-permute-start | bytes 1544 | tf_op jit(solution)/shard_map/ppermute | solution.py:588
